TPU v7x, 512 devices: a whole 4x8x8 slice. The times are simulated.
512 devices in a mesh: row: 32 (over x, y), col: 16 (over z, core).
Axes of the slice: x: 4, y: 8, z: 8, core: 2. Of those that a mesh axis runs over, the one named last changes fastest.
Arguments:
- k_vals: float32 [512, 15, 64, 64], P('row'), may hold values from -0.1875 to 0.1875
- k_cols: int32 [512, 15], P('row'), may hold values from -8 to 519, as said below
- p_vals: float32 [512, 3, 64, 64], P('row', None, None, 'col'), may hold values from -1.2 to 1.2
- p_cols: int32 [512, 3], P('row'), may hold values from -1 to 63, as said below
Outputs:
- coarse: float32 [64, 7, 64, 64], P('row', None, None, 'col')
Inputs may be any that keep to these rules, and one draw needn't show every extreme that they name: Each k_cols[i, s] - i lies between -8 and 8; within a block row the columns differ; a column outside 0 to 511 stands for an absent block. Each p_cols[k, s] is -1 for an absent block or lies within 1 of k // 8, the aggregate of block row k; the present columns of a row differ, and the aggregate of every block row is present.
All inputs are finite; a program needn't handle non-finite values.
Results may differ from a plain program's by a relative error of at most 0.0001.
Values sent between devices are 32-bit elements; how exact they have to be, the bound alone decides.
A program may use at most 128 MiB of HBM per device.

v0:
```python
import jax
import jax.numpy as jnp
from jax import lax
from jax.sharding import PartitionSpec as P

AGG = 8


def extended_2(cells, sides, width):
    for axis, dim in sides:
        count = lax.axis_size(axis)
        ends = count - 1
        head = lax.slice_in_dim(cells, 0, width, axis=dim)
        tail = lax.slice_in_dim(cells, cells.shape[dim] - width, cells.shape[dim], axis=dim)
        cells = jnp.concatenate(
            [
                lax.ppermute(tail, axis, [(i, (i + 1) % count) for i in range(ends)]),
                cells,
                lax.ppermute(head, axis, [((i + 1) % count, i) for i in range(ends)]),
            ],
            axis=dim,
        )
    return cells


def place_window(p_vals, p_cols, aggregate, blocks_all):
    present = (p_cols >= 0) & (p_cols < blocks_all)
    position = p_cols - aggregate[:, None] + 1
    selector = (
        (position[:, :, None] == jnp.arange(3, dtype=jnp.int32)[None, None, :])
        & present[:, :, None]
    ).astype(jnp.float32)
    return jnp.einsum("jtu,jtbc->jubc", selector, p_vals, precision=lax.Precision.HIGHEST)


def stiff_rows(blocks, columns, first_row, padded, margin, total_rows):
    count = blocks.shape[0]
    fine_width = blocks.shape[2]
    share = padded.shape[3]
    aggregate = (first_row + jnp.arange(count, dtype=jnp.int32)) // AGG
    in_range = (columns >= 0) & (columns < total_rows)
    safe_cols = jnp.clip(columns, 0, total_rows - 1)
    near_agg = safe_cols // AGG - aggregate[:, None] + 1
    side_mask = (
        (near_agg[:, :, None] == jnp.arange(3, dtype=jnp.int32)[None, None, :])
        & in_range[:, :, None]
    ).astype(jnp.float32)
    local_cols = jnp.clip(columns - first_row + margin, 0, padded.shape[0] - 1)
    picked = jnp.take(padded, local_cols, axis=0)
    product = jnp.einsum("isab,isubc->isuac", blocks, picked, precision=lax.Precision.HIGHEST)
    mixed_terms = jnp.einsum(
        "ise,isuac->ieuac", side_mask, product, precision=lax.Precision.HIGHEST
    )
    result = jnp.zeros((count, 5, fine_width, share), jnp.float32)
    for offset in range(3):
        result = result.at[:, offset : offset + 3].add(mixed_terms[:, offset])
    return result


def make_partial(stiff_prolong, column_piece):
    count = stiff_prolong.shape[0]
    groups = count // AGG
    share = stiff_prolong.shape[3]
    upper_side = stiff_prolong.reshape(groups, AGG, 5, stiff_prolong.shape[2], share)
    lower_side = column_piece.reshape(groups, AGG, 3, column_piece.shape[2], column_piece.shape[3])
    grouped = jnp.einsum(
        "giubc,giwbd->guwcd", lower_side, upper_side, precision=lax.Precision.HIGHEST
    )
    partial_value = jnp.zeros((groups + 2, 7, column_piece.shape[3], share), jnp.float32)
    for left_slot in range(3):
        for right_slot in range(5):
            partial_value = partial_value.at[
                left_slot : left_slot + groups, right_slot - left_slot + 2
            ].add(grouped[:, left_slot, right_slot])
    return partial_value


def body(k_vals, k_cols, p_vals, p_cols):
    own_rows = k_vals.shape[0]
    groups = own_rows // AGG
    total_rows = own_rows * lax.axis_size("row")
    blocks_all = total_rows // AGG
    first_row = lax.axis_index("row") * own_rows
    aggregate = (first_row + jnp.arange(own_rows, dtype=jnp.int32)) // AGG
    window = place_window(p_vals, p_cols, aggregate, blocks_all)
    extended = extended_2(window, (("row", 0),), AGG)
    stiff_prolong = stiff_rows(k_vals, k_cols, first_row, extended, AGG, total_rows)
    terms = make_partial(stiff_prolong, lax.all_gather(window, "col", axis=3, tiled=True))
    bordered = extended_2(terms, (("row", 0),), 1)
    coarse = terms[1 : groups + 1]
    coarse = coarse.at[0].add(bordered[0])
    coarse = coarse.at[groups - 1].add(bordered[groups + 3])
    return coarse


def solution(mesh):
    placed = (
        P("row", None, None, None),
        P("row", None),
        P("row", None, None, "col"),
        P("row", None),
    )
    return jax.shard_map(
        body, mesh=mesh, in_specs=placed, out_specs=P("row", None, None, "col"), check_vma=False
    )
```

profile of v0, /device:TPU:24, one launch (start us, length us, event | category | flops | bytes accessed | tf_op | source)
XLA Modules:
  0.0 88.2 jit_solution(9705422812742580384)
XLA Ops:
  0.0 0.0 copy-start
  0.0 0.0 copy-start.2
  0.0 0.7 compare_and_fusion.2
  0.7 0.7 subtract_add_fusion
  1.4 0.1 copy.5
  1.5 0.1 copy.6
  1.6 0.0 copy-done
  1.6 0.3 fusion.14
  1.9 4.7 %collective-permute-start = (f32[8,3,64,4]{2,1,3,0:T(4,128)S(1)}, f32[8,3,64,4]{2,1,3,0:T(4,128)S(1)}, u32[]{:S(2)}, u32[]{:S(2)}) collective-permute-start(f32[8,3,64,4]{2,1,3,0:T(4,128)S(1)} %get-tuple-element.254), channel_id=1, source_target_pairs={{0,16},{16,32},{32,48},{48,64},{64,80},{80,96},{96,112},{112,128},... | collective-permute-start | bytes 73736 | tf_op jit(solution)/shard_map/ppermute | solution.py:17
  6.6 1.9 %collective-permute-start.1 = (f32[8,3,64,4]{2,1,3,0:T(4,128)S(1)}, f32[8,3,64,4]{2,1,3,0:T(4,128)S(1)}, u32[]{:S(2)}, u32[]{:S(2)}) collective-permute-start(f32[8,3,64,4]{2,1,3,0:T(4,128)S(1)} %get-tuple-element.255), channel_id=1, source_target_pairs={{16,0},{32,16},{48,32},{64,48},{80,64},{96,80},{112,96},{128,112},... | collective-permute-start | bytes 73736 | tf_op jit(solution)/shard_map/ppermute | solution.py:19
  8.5 0.7 compare_and_fusion
  9.3 0.8 fusion.31
  10.0 30.3 %all_gather.3 = f32[16,3,64,64]{2,1,3,0:T(4,128)} all-gather(f32[16,3,64,4]{2,1,3,0:T(4,128)S(1)} %fusion.14), channel_id=1, replica_groups=mesh['row'=32,'col'=16] {'col'}, dimensions={3}, use_global_device_ids=true | all-gather | bytes 835584 | tf_op jit(solution)/shard_map/all_gather | solution.py:88
  40.3 0.6 fusion.42
  40.9 0.6 fusion.41
  41.6 0.6 fusion.40
  42.2 0.6 fusion.39
  42.8 0.0 copy-done.2
  42.8 0.7 and_reduce_fusion.4
  43.5 0.8 and_reduce_fusion
  44.3 0.6 fusion.38
  44.9 0.1 reshape.885
  45.0 0.0 collective-permute-done
  45.0 0.0 collective-permute-done.1
  45.1 0.1 pad_maximum_fusion
  45.1 1.8 %gather_fusion = f32[240,3,64,4]{2,1,3,0:T(4,128)S(1)} fusion(f32[32,3,64,4]{2,1,3,0:T(4,128)S(1)} %pad_maximum_fusion, s32[1024]{0:T(1024)S(1)} %pad_clamp_fusion), kind=kCustom, calls=%fused_computation | custom fusion | bytes 1475520 | tf_op jit(solution)/shard_map/jit(_take)/gather | solution.py:49
  46.9 15.4 %fusion = f32[16,15,3,4,64]{4,2,3,1,0:T(4,128)S(1)} fusion(f32[16,15,64,64]{3,2,1,0:T(8,128)} %param.44, f32[16,15,3,64,4]{3,2,4,1,0:T(4,128)S(1)} %bitcast.90, pred[16,15]{1,0:T(8,128)(4,1)S(1)} %get-tuple-element.249), kind=kOutput, calls=%fused_computation.1 | convolution fusion | flops 141742080 | bytes 5406960 | tf_op jit(solution)/shard_map/isab,isubc->isuac/dot_general | solution.py:50
  62.4 0.0 copy-start.1
  62.4 1.1 %fusion.5 = f32[16,3,3,64,4]{3,1,4,2,0:T(4,128)S(1)} fusion(f32[16,15,3,4,64]{4,2,3,1,0:T(4,128)S(1)} %fusion, s32[16,15]{1,0:T(8,128)S(1)} %fusion.31, pred[16,15]{1,0:T(8,128)(4,1)S(1)} %get-tuple-element.273), kind=kOutput, calls=%fused_computation.6 | convolution fusion | flops 6636960 | bytes 885936 | tf_op jit(solution)/shard_map/ise,isuac->ieuac/dot_general | solution.py:51
  63.4 0.2 fusion.34
  63.8 0.2 copy-done.1
  64.0 1.9 %fusion.8 = f32[2,3,5,64,4]{3,2,1,4,0:T(8,128)S(1)} fusion(f32[2,8,3,64,64,1]{3,2,4,1,0,5:T(4,128)S(1)} %bitcast.91, f32[2,8,5,64,4,1]{3,4,2,1,0,5:T(4,128)S(1)} %bitcast.92), kind=kOutput, calls=%fused_computation.9 | convolution fusion | flops 47185920 | bytes 899072 | tf_op jit(solution)/shard_map/giubc,giwbd->guwcd/dot_general | solution.py:66
  65.9 1.9 %constant_dynamic-update-slice_fusion.14 = f32[4,7,64,4]{2,3,0,1:T(4,128)S(1)} fusion(f32[4,7,64,4]{2,3,0,1:T(4,128)S(1)} %broadcast_in_dim.11, s32[]{:T(128)} %bitcast.19, s32[]{:T(128)} %bitcast.20, f32[2,1,1,64,4]{3,4,0,2,1:T(4,128)S(1)} %bitcast.110, pred[]{:T(512)} %and_reduce_fusion.4), kind=kLoop, calls=%fused_computation.67 | loop fusion | flops 512 | bytes 8201 | tf_op jit(solution)/shard_map/scatter-add | solution.py:74
  67.8 2.0 %constant_dynamic-update-slice_fusion.13 = f32[4,7,64,4]{2,3,0,1:T(4,128)S(1)} fusion(f32[4,7,64,4]{2,3,0,1:T(4,128)S(1)} %constant_dynamic-update-slice_fusion.14, s32[]{:T(128)} %bitcast.21, s32[]{:T(128)} %bitcast.22, f32[2,1,64,4]{2,3,0,1:T(4,128)S(1)} %bitcast.109, pred[]{:T(512)} %get-tuple-element.276), kind=kLoop, calls=%fused_computation.65 | loop fusion | flops 1024 | bytes 12297 | tf_op jit(solution)/shard_map/scatter-add | solution.py:74
  69.8 1.9 %constant_dynamic-update-slice_fusion.12 = f32[4,7,64,4]{2,3,0,1:T(4,128)S(1)} fusion(f32[4,7,64,4]{2,3,0,1:T(4,128)S(1)} %constant_dynamic-update-slice_fusion.13, s32[]{:T(128)} %bitcast.25, s32[]{:T(128)} %bitcast.26, f32[2,1,64,4]{2,3,0,1:T(4,128)S(1)} %bitcast.108, pred[]{:T(512)} %get-tuple-element.277), kind=kLoop, calls=%fused_computation.63 | loop fusion | flops 1024 | bytes 12297 | tf_op jit(solution)/shard_map/scatter-add | solution.py:74
  71.8 1.9 %constant_dynamic-update-slice_fusion.11 = f32[4,7,64,4]{2,3,0,1:T(4,128)S(1)} fusion(f32[4,7,64,4]{2,3,0,1:T(4,128)S(1)} %constant_dynamic-update-slice_fusion.12, s32[]{:T(128)} %bitcast.28, s32[]{:T(128)} %bitcast.29, f32[2,1,64,4]{2,3,0,1:T(4,128)S(1)} %bitcast.107, pred[]{:T(512)} %get-tuple-element.246), kind=kLoop, calls=%fused_computation.61 | loop fusion | flops 1024 | bytes 12297 | tf_op jit(solution)/shard_map/scatter-add | solution.py:74
  73.7 1.7 %constant_dynamic-update-slice_fusion.10 = f32[4,7,64,4]{2,3,0,1:T(4,128)S(1)} fusion(f32[4,7,64,4]{2,3,0,1:T(4,128)S(1)} %constant_dynamic-update-slice_fusion.11, s32[]{:T(128)} %bitcast.31, s32[]{:T(128)} %bitcast.32, f32[2,1,64,4]{2,3,0,1:T(4,128)S(1)} %bitcast.106, pred[]{:T(512)} %get-tuple-element.245), kind=kLoop, calls=%fused_computation.59 | loop fusion | flops 1024 | bytes 12297 | tf_op jit(solution)/shard_map/scatter-add | solution.py:74
  75.5 5.1 %collective-permute-start.2 = (f32[1,7,64,4]{2,3,0,1:T(4,128)S(1)}, f32[1,7,64,4]{2,3,0,1:T(4,128)S(1)}, u32[]{:S(2)}, u32[]{:S(2)}) collective-permute-start(f32[1,7,64,4]{2,3,0,1:T(4,128)S(1)} %get-tuple-element.272), channel_id=1, source_target_pairs={{0,16},{16,32},{32,48},{48,64},{64,80},{80,96},{96,112},{112,128},... | collective-permute-start | bytes 21512 | tf_op jit(solution)/shard_map/ppermute | solution.py:17
  80.7 1.9 %collective-permute-start.3 = (f32[1,7,64,4]{2,3,0,1:T(4,128)S(1)}, f32[1,7,64,4]{2,3,0,1:T(4,128)S(1)}, u32[]{:S(2)}, u32[]{:S(2)}) collective-permute-start(f32[1,7,64,4]{2,3,0,1:T(4,128)S(1)} %get-tuple-element.271), channel_id=1, source_target_pairs={{16,0},{32,16},{48,32},{64,48},{80,64},{96,80},{112,96},{128,112},... | collective-permute-start | bytes 21512 | tf_op jit(solution)/shard_map/ppermute | solution.py:19
  82.6 0.0 collective-permute-done.2
  82.7 4.9 %collective-permute-done.3 = f32[1,7,64,4]{2,3,0,1:T(4,128)S(1)} collective-permute-done((f32[1,7,64,4]{2,3,0,1:T(4,128)S(1)}, f32[1,7,64,4]{2,3,0,1:T(4,128)S(1)}, u32[]{:S(2)}, u32[]{:S(2)}) %collective-permute-start.3) | collective-permute-done | bytes 7200 | tf_op jit(solution)/shard_map/ppermute | solution.py:19
  87.5 0.6 copy.26
  (25 shorter events, 0.3 us)
Async XLA Ops:
  0.0 1.6 %copy-start = (f32[16,3,64,4]{2,3,1,0:T(4,128)S(1)}, f32[16,3,64,4]{2,3,1,0:T(4,128)}, u32[]{:S(2)}) copy-start(f32[16,3,64,4]{2,3,1,0:T(4,128)} %param.46) | copy-start | bytes 147460
  0.0 42.8 %copy-start.2 = (s32[4]{0:T(128)S(1)}, s32[4]{0:T(128)}, u32[]{:S(2)}) copy-start(s32[4]{0:T(128)} %constant.605.clone.1) | copy-start | bytes 52
  1.9 43.1 %collective-permute-start = (f32[8,3,64,4]{2,1,3,0:T(4,128)S(1)}, f32[8,3,64,4]{2,1,3,0:T(4,128)S(1)}, u32[]{:S(2)}, u32[]{:S(2)}) collective-permute-start(f32[8,3,64,4]{2,1,3,0:T(4,128)S(1)} %get-tuple-element.254), channel_id=1, source_target_pairs={{0,16},{16,32},{32,48},{48,64},{64,80},{80,96},{96,112},{112,128},... | collective-permute-start | bytes 73736 | tf_op jit(solution)/shard_map/ppermute | solution.py:17
  6.6 38.4 %collective-permute-start.1 = (f32[8,3,64,4]{2,1,3,0:T(4,128)S(1)}, f32[8,3,64,4]{2,1,3,0:T(4,128)S(1)}, u32[]{:S(2)}, u32[]{:S(2)}) collective-permute-start(f32[8,3,64,4]{2,1,3,0:T(4,128)S(1)} %get-tuple-element.255), channel_id=1, source_target_pairs={{16,0},{32,16},{48,32},{64,48},{80,64},{96,80},{112,96},{128,112},... | collective-permute-start | bytes 73736 | tf_op jit(solution)/shard_map/ppermute | solution.py:19
  62.4 1.6 %copy-start.1 = (f32[16,3,64,64]{2,1,3,0:T(4,128)S(1)}, f32[16,3,64,64]{2,1,3,0:T(4,128)}, u32[]{:S(2)}) copy-start(f32[16,3,64,64]{2,1,3,0:T(4,128)} %all_gather.3) | copy-start | bytes 2359300
  75.5 7.1 %collective-permute-start.2 = (f32[1,7,64,4]{2,3,0,1:T(4,128)S(1)}, f32[1,7,64,4]{2,3,0,1:T(4,128)S(1)}, u32[]{:S(2)}, u32[]{:S(2)}) collective-permute-start(f32[1,7,64,4]{2,3,0,1:T(4,128)S(1)} %get-tuple-element.272), channel_id=1, source_target_pairs={{0,16},{16,32},{32,48},{48,64},{64,80},{80,96},{96,112},{112,128},... | collective-permute-start | bytes 21512 | tf_op jit(solution)/shard_map/ppermute | solution.py:17
  80.7 6.8 %collective-permute-start.3 = (f32[1,7,64,4]{2,3,0,1:T(4,128)S(1)}, f32[1,7,64,4]{2,3,0,1:T(4,128)S(1)}, u32[]{:S(2)}, u32[]{:S(2)}) collective-permute-start(f32[1,7,64,4]{2,3,0,1:T(4,128)S(1)} %get-tuple-element.271), channel_id=1, source_target_pairs={{16,0},{32,16},{48,32},{64,48},{80,64},{96,80},{112,96},{128,112},... | collective-permute-start | bytes 21512 | tf_op jit(solution)/shard_map/ppermute | solution.py:19
where the time goes:
time: 88.6 us; the launch traced here: 88.2 us
  blocking collectives  30.3 us (34%)
  matrix products  18.7 us (21%)
  other arithmetic  14.2 us (16%)
  starting transfers between devices  13.7 us (15%)
  local copies, waits for them, and re-layouts  6.23 us (7%)
  waiting for transfers between devices  4.87 us (5%)
    all_gather x1, blocking collectives, body(): lax.all_gather(window, 'col', axis=3, tiled=True)  30.3 us
    dot_general x1, matrix products, stiff_rows(): jnp.einsum('isab,isubc->isuac', blocks, picked, precision=lax.Precision.H...  15.4 us
    ppermute x2, starting transfers between devices, extended_2(): lax.ppermute(tail, axis, [(i, (i + 1) % count) for i in range(ends)])  9.84 us
    scatter-add x15, other arithmetic, make_partial(): partial_value = partial_value.at[left_slot:left_slot + groups, right_slot...  9.55 us
    ppermute x2, waiting for transfers between devices, extended_2(): lax.ppermute(head, axis, [((i + 1) % count, i) for i in range(ends)])  4.87 us
    ppermute x2, starting transfers between devices, extended_2(): lax.ppermute(head, axis, [((i + 1) % count, i) for i in range(ends)])  3.84 us
    another operation x5, local copies, waits for them, and re-layouts  3.06 us
    dot_general x1, matrix products, make_partial(): jnp.einsum('giubc,giwbd->guwcd', lower_side, upper_side, precision=lax.Pr...  1.9 us
  transfers between devices with their start and end apart: 4, of which 1 were waited for; matrix products, arithmetic and copies ran while one was open for 7% of the time, Pallas kernels for 0%

commit v1 on v0

v1 whole, which is shorter than its diff:
```python
import functools

import jax
import jax.numpy as jnp
from jax import lax
from jax.experimental import pallas as pl
from jax.experimental.pallas import tpu as pltpu
from jax.sharding import PartitionSpec as P

AGG = 8
RING = 8
MESH = pl.DeviceIdType.MESH
F32 = jnp.float32
BF16 = jnp.bfloat16


def kernel(
    row_count,
    p_cols,
    k_cols,
    p_hbm,
    k_hbm,
    out,
    p_buf,
    k_buf,
    k_split,
    chunk,
    ring,
    halo_out,
    halo_in,
    table,
    weights,
    left_side,
    terms,
    mine,
    side_out,
    side_in,
    final,
    p_sem,
    k_sem,
    ring_send,
    ring_recv,
    pair_sem,
    halo_send,
    halo_recv,
    side_send,
    side_recv,
):
    row = lax.axis_index("row")
    col = lax.axis_index("col")
    z = lax.div(col, 2)
    core = lax.rem(col, 2)
    right = (row, lax.rem(z + 1, RING) * 2 + core)
    left = (row, lax.rem(z + RING - 1, RING) * 2 + core)
    twin = (row, z * 2 + 1 - core)
    above = [(lax.rem(row + 1, row_count), z * 2 + n) for n in range(2)]
    below = [(lax.rem(row + row_count - 1, row_count), z * 2 + n) for n in range(2)]
    peers = [right, left, twin] + above + below

    barrier = pltpu.get_barrier_semaphore()
    for peer in peers:
        pl.semaphore_signal(barrier, inc=1, device_id=peer, device_id_type=MESH)
    p_copy = pltpu.make_async_copy(p_hbm, p_buf, p_sem)
    p_copy.start()
    k_copies = []
    for part in range(4):
        rows = pl.ds(4 * part, 4)
        k_copies.append(pltpu.make_async_copy(k_hbm.at[rows], k_buf.at[rows], k_sem.at[part]))
        k_copies[-1].start()

    own_rows = 2 * AGG
    first_row = row * own_rows
    total_rows = row_count * own_rows
    blocks_all = total_rows // AGG
    top = lax.broadcasted_iota(jnp.int32, (8, 128), 0) < 4
    low = lax.broadcasted_iota(jnp.int32, (8, 128), 1) < 64

    def swap_rows(value):
        return pltpu.roll(value, 4, 0)

    def swap_lanes(value):
        return pltpu.roll(value, 64, 1)

    p_copy.wait()

    def window(j, u):
        total = jnp.zeros((4, 64), F32)
        for t in range(3):
            block = p_cols[t, j]
            position = block - (2 * row + j // AGG) + 1
            position = jnp.where((block >= 0) & (block < blocks_all), position, -1)
            total = total + jnp.where(jnp.full((4, 64), position) == u, p_buf[j, t], 0.0)
        return total

    for m in range(4):
        for u in range(3):
            halves = [
                jnp.concatenate([window(g * AGG + 2 * m, u), window(g * AGG + 2 * m + 1, u)], axis=1)
                for g in range(2)
            ]
            chunk[core, m * 3 + u] = jnp.concatenate(halves, axis=0)
    for m in range(2):
        for u in range(3):
            even, odd = chunk[core, 2 * m * 3 + u], chunk[core, (2 * m + 1) * 3 + u]
            mixed = swap_rows(jnp.where(top, odd, even))
            halo_out[0, m * 3 + u] = jnp.where(top, even, mixed)
            halo_out[1, m * 3 + u] = jnp.where(top, mixed, odd)

    pl.semaphore_wait(barrier, len(peers))

    def ring_copy(way, step, half):
        part = pl.ds(6 * half, 6)
        slot = 7 - step if way == 0 else 1 + step
        before = slot + 1 if way == 0 else slot - 1
        source = chunk.at[core, part] if step == 0 else ring.at[before, part]
        return pltpu.make_async_remote_copy(
            src_ref=source,
            dst_ref=ring.at[slot, part],
            send_sem=ring_send.at[way, step, half],
            recv_sem=ring_recv.at[way, step, half],
            device_id=right if way == 0 else left,
            device_id_type=MESH,
        )

    started = []
    ring_copies = {}

    def send_ring(step, half):
        for way in range(2):
            if step < 3 or way == half:
                copy = ring_copy(way, step, half)
                copy.start()
                started.append(copy)
                ring_copies[way, step, half] = copy

    def take_ring(step, half):
        for way in range(2):
            if step < 3 or way == half:
                ring_copies[way, step, half].wait_recv()

    for half in range(2):
        send_ring(0, half)
    pair_copy = pltpu.make_async_remote_copy(
        src_ref=chunk.at[core],
        dst_ref=chunk.at[core],
        send_sem=pair_sem.at[0],
        recv_sem=pair_sem.at[1],
        device_id=twin,
        device_id_type=MESH,
    )
    pair_copy.start()

    def halo_copy(way, n, sender):
        return pltpu.make_async_remote_copy(
            src_ref=halo_out.at[way],
            dst_ref=halo_in.at[way, sender],
            send_sem=halo_send.at[way, n],
            recv_sem=halo_recv.at[way, sender],
            device_id=(below if way == 0 else above)[n],
            device_id_type=MESH,
        )

    for way in range(2):
        for n in range(2):
            copy = halo_copy(way, n, core)
            copy.start()
            started.append(copy)

    def split_k(i, carry):
        for q in range(4):
            pairs = []
            for s in (4 * q, 4 * q + 2):
                second = k_buf[i, s + 1] if s + 1 < 15 else jnp.zeros((64, 64), F32)
                pairs.append(jnp.concatenate([k_buf[i, s], second], axis=1))
            both = jnp.concatenate(pairs, axis=1)
            high = both.astype(BF16)
            k_split[i, q, 0:64] = high
            k_split[i, q, 64:128] = (both - high.astype(F32)).astype(BF16)
        return carry

    def split_part(part):
        k_copies[part].wait()
        lax.fori_loop(4 * part, 4 * part + 4, split_k, 0)

    split_part(0)
    split_part(1)
    take_ring(0, 0)
    send_ring(1, 0)
    take_ring(0, 1)
    send_ring(1, 1)
    split_part(2)
    split_part(3)

    def merge(zero, one):
        mixed = swap_rows(jnp.where(top, one, zero))
        return jnp.where(top, zero, mixed), jnp.where(top, mixed, one)

    def place(pair, side, tiles):
        for flipped in range(2):
            blocks = [swap_lanes(tile) for tile in tiles] if flipped else list(tiles)
            if side > 0:
                blocks = [jnp.zeros((8 * side, 128), F32)] + blocks
            if side < 3:
                blocks = blocks + [jnp.zeros((8 * (3 - side), 128), F32)]
            whole = jnp.concatenate(blocks, axis=0)
            high = whole.astype(BF16)
            table[2 * pair + flipped, 0] = high
            table[2 * pair + flipped, 1] = (whole - high.astype(F32)).astype(BF16)

    pair_copy.wait_recv()
    table[32:34] = jnp.zeros((2, 2, 48, 128), BF16)

    def place_own(m, carry):
        merged = [merge(chunk[0, m * 3 + u], chunk[1, m * 3 + u]) for u in range(3)]
        for g in range(2):
            place(4 + 4 * g + m, 1 + g, [merged[u][g] for u in range(3)])
        return carry

    lax.fori_loop(0, 4, place_own, 0)
    for way in range(2):
        for n in range(2):
            halo_copy(way, n, n).wait_recv()

    def place_halo(m, carry):
        for way, base, side in ((1, 0, 0), (0, 12, 3)):
            merged = [merge(halo_in[way, 0, m * 3 + u], halo_in[way, 1, m * 3 + u]) for u in range(3)]
            for x in range(2):
                place(base + 2 * m + x, side, [merged[u][x] for u in range(3)])
        return carry

    lax.fori_loop(0, 2, place_halo, 0)
    take_ring(1, 0)
    send_ring(2, 0)
    take_ring(1, 1)
    send_ring(2, 1)

    def entry(i, s):
        if s >= 15:
            return 32
        block = k_cols[i, s]
        near = block - first_row + AGG
        inside = (block >= 0) & (block < total_rows) & (near >= 0) & (near < 32)
        return jnp.where(inside, near, 32)

    low_16 = lax.broadcasted_iota(jnp.int32, (48, 128), 1) < 64
    blank = jnp.zeros((16, 128), BF16)

    def multiply_row(i, group):
        total = None
        for q in range(4):
            sides = []
            for s in (4 * q, 4 * q + 2):
                even = entry(i, s)
                odd = lax.bitwise_xor(entry(i, s + 1), 1)
                parts = [
                    jnp.where(low_16, table[even, part], table[odd, part]) for part in range(2)
                ]
                if group == 1:
                    parts = parts[::-1]
                sides.append(jnp.concatenate([parts[0], blank, parts[1], blank], axis=0))
            term = lax.dot_general(
                k_split[i, q],
                jnp.concatenate(sides, axis=1),
                (((1,), (1,)), ((), ())),
                preferred_element_type=F32,
            )
            total = term if total is None else total + term
        return total[0:64], total[64:128]

    low_64 = lax.broadcasted_iota(jnp.int32, (64, 128), 1) < 64

    def multiply(i, carry):
        a_0, b_0 = multiply_row(i, 0)
        a_1, b_1 = multiply_row(i + AGG, 1)
        value = jnp.where(low_64, a_0 + b_0, a_1 + b_1)
        value = value + swap_lanes(jnp.where(low_64, a_1, a_0))
        high = value.astype(BF16)
        rows = pl.ds(pl.multiple_of(64 * i, 64), 64)
        weights[rows, 0:128] = high
        weights[rows, 128:256] = (value - high.astype(F32)).astype(BF16)
        return carry

    lax.fori_loop(0, 4, multiply, 0)
    take_ring(2, 0)
    send_ring(3, 0)
    take_ring(2, 1)
    send_ring(3, 1)
    lax.fori_loop(4, 8, multiply, 0)

    order = (0, 1, 7, 2, 6, 3, 5, 4)

    def prepare(place_at, slot):
        def tile(m, u):
            return chunk[core, m * 3 + u] if slot == 0 else ring[slot, m * 3 + u]

        whole = jnp.concatenate(
            [jnp.concatenate([tile(m, u) for m in range(4)], axis=1) for u in range(3)], axis=0
        )
        rest = whole - whole.astype(BF16).astype(F32)
        left_side[pl.ds(48 * place_at, 48)] = jnp.concatenate([whole, rest], axis=0).astype(BF16)

    def products(first, count):
        result = lax.dot_general(
            left_side[pl.ds(48 * first, 48 * count)],
            weights[...],
            (((1,), (0,)), ((), ())),
            preferred_element_type=F32,
        )
        for n in range(count):
            base = 48 * n
            folded = []
            for u in range(3):
                a = base + 8 * u
                value = result[a : a + 8, 0:128] + result[a : a + 8, 128:256]
                value = value + result[a + 24 : a + 32, 0:128]
                folded.append(jnp.where(top, value, swap_lanes(value)))
            middle = folded[1] + swap_rows(jnp.where(top, folded[2], folded[0]))
            outer = jnp.where(top, folded[0], folded[2])
            slot = order[first + n]
            terms[0, slot] = jnp.where(top, pltpu.roll(middle, 8, 1), middle)
            terms[1, slot] = jnp.where(top, pltpu.roll(outer, 16, 1), pltpu.roll(outer, 120, 1))

    for n in range(5):
        prepare(n, order[n])
    products(0, 5)
    for n in range(5, 7):
        prepare(n, order[n])
    take_ring(3, 0)
    take_ring(3, 1)
    prepare(7, order[7])
    products(5, 3)

    def packed(kind, t):
        return jnp.where(low, terms[kind, t], swap_lanes(terms[kind, t + 4]))

    for t in range(4):
        mine[core, t] = packed(0, t)
    for t in range(2):
        one, two = packed(1, t), packed(1, t + 2)
        side_out[0, t] = jnp.where(top, one, swap_rows(two))
        side_out[1, t] = jnp.where(top, swap_rows(one), two)

    def side_copy(way, n, sender):
        return pltpu.make_async_remote_copy(
            src_ref=side_out.at[way],
            dst_ref=side_in.at[way, sender],
            send_sem=side_send.at[way, n],
            recv_sem=side_recv.at[way, sender],
            device_id=(below if way == 0 else above)[n],
            device_id_type=MESH,
        )

    for way in range(2):
        for n in range(2):
            copy = side_copy(way, n, core)
            copy.start()
            started.append(copy)
    twin_copy = pltpu.make_async_remote_copy(
        src_ref=mine.at[core],
        dst_ref=mine.at[core],
        send_sem=pair_sem.at[2],
        recv_sem=pair_sem.at[3],
        device_id=twin,
        device_id_type=MESH,
    )
    twin_copy.start()
    for copy in started:
        copy.wait_send()
    pair_copy.wait_send()
    twin_copy.wait()
    for way in range(2):
        for n in range(2):
            side_copy(way, n, n).wait_recv()

    for t in range(4):
        sums = []
        for n in range(2):
            up, down = side_in[1, n, t % 2], side_in[0, n, t % 2]
            if t < 2:
                other = jnp.where(top, up, swap_rows(down))
            else:
                other = jnp.where(top, swap_rows(up), down)
            sums.append(mine[n, t] + other)
        first = jnp.where(top, sums[0], swap_rows(sums[1]))
        second = jnp.where(top, swap_rows(sums[0]), sums[1])
        final[lax.rem(z + t, RING)] = jnp.where(low, first, swap_lanes(second))
        final[lax.rem(z + t + 4, RING)] = jnp.where(low, swap_lanes(first), second)
    turned = jnp.transpose(jnp.concatenate([final[n] for n in range(RING)], axis=0))
    even_core = jnp.full((4, 64), core) == 0
    for block in range(2):
        for band in range(7):
            a = 64 * block + 8 * band
            out[block, band] = jnp.where(even_core, turned[a : a + 4], turned[a + 4 : a + 8])


def body(row_count, k_vals, k_cols, p_vals, p_cols):
    own = k_vals.shape[0]
    dma = pltpu.SemaphoreType.DMA
    result = pl.pallas_call(
        functools.partial(kernel, row_count),
        out_shape=jax.ShapeDtypeStruct((2, 7, 4, 64), F32),
        in_specs=[
            pl.BlockSpec(memory_space=pltpu.SMEM),
            pl.BlockSpec(memory_space=pltpu.SMEM),
            pl.BlockSpec(memory_space=pl.ANY),
            pl.BlockSpec(memory_space=pl.ANY),
        ],
        out_specs=pl.BlockSpec(memory_space=pltpu.VMEM),
        scratch_shapes=[
            pltpu.VMEM((own, 3, 4, 64), F32),
            pltpu.VMEM((own, 15, 64, 64), F32),
            pltpu.VMEM((own, 4, 128, 256), BF16),
            pltpu.VMEM((2, 12, 8, 128), F32),
            pltpu.VMEM((RING, 12, 8, 128), F32),
            pltpu.VMEM((2, 6, 8, 128), F32),
            pltpu.VMEM((2, 2, 6, 8, 128), F32),
            pltpu.VMEM((34, 2, 48, 128), BF16),
            pltpu.VMEM((512, 256), BF16),
            pltpu.VMEM((384, 512), BF16),
            pltpu.VMEM((2, RING, 8, 128), F32),
            pltpu.VMEM((2, 4, 8, 128), F32),
            pltpu.VMEM((2, 2, 8, 128), F32),
            pltpu.VMEM((2, 2, 2, 8, 128), F32),
            pltpu.VMEM((RING, 8, 128), F32),
            dma,
            dma((4,)),
            dma((2, 4, 2)),
            dma((2, 4, 2)),
            dma((4,)),
            dma((2, 2)),
            dma((2, 2)),
            dma((2, 2)),
            dma((2, 2)),
        ],
        compiler_params=pltpu.CompilerParams(
            collective_id=0, has_side_effects=True, vmem_limit_bytes=40 * 1024 * 1024
        ),
    )(jnp.transpose(p_cols), k_cols, jnp.transpose(p_vals, (0, 1, 3, 2)), k_vals)
    return jnp.transpose(result, (0, 1, 3, 2))


def solution(mesh):
    placed = (
        P("row", None, None, None),
        P("row", None),
        P("row", None, None, "col"),
        P("row", None),
    )
    return jax.shard_map(
        functools.partial(body, mesh.shape["row"]),
        mesh=mesh,
        in_specs=placed,
        out_specs=P("row", None, None, "col"),
        check_vma=False,
    )
```

time: 88.6 us -> 40 us (0.45)
  the two profiles are of different devices: /device:TPU:24 before, /device:TPU:1 now
where the time goes in v1:
time: 40 us; the launch traced here: 39.8 us
  Pallas kernels  33.7 us (84%)
  local copies, waits for them, and re-layouts  6.11 us (15%)
    pallas_call x1, Pallas kernels, body(): pl.pallas_call(functools.partial(kernel, row_count), out_shape=jax.ShapeD...  33.7 us
    unnamed x9, local copies, waits for them, and re-layouts  6.11 us

profile of v1, /device:TPU:1, one launch (start us, length us, event | category | flops | bytes accessed | tf_op | source)
XLA Modules:
  0.0 39.8 jit_solution(601808491604184044)
XLA Ops:
  0.0 0.0 copy-start
  0.0 3.2 %copy-done = f32[16,15,64,64]{3,2,1,0:T(8,128)S(1)} copy-done((f32[16,15,64,64]{3,2,1,0:T(8,128)S(1)}, f32[16,15,64,64]{3,2,1,0:T(8,128)}, u32[]{:S(2)}) %copy-start) | copy-done | bytes 3932184
  3.2 0.0 copy-start.1
  3.2 0.9 %copy-done.1 = f32[16,3,64,4]{2,3,1,0:T(4,128)S(1)} copy-done((f32[16,3,64,4]{2,3,1,0:T(4,128)S(1)}, f32[16,3,64,4]{2,3,1,0:T(4,128)}, u32[]{:S(2)}) %copy-start.1) | copy-done | bytes 49176
  4.1 0.0 copy-start.2
  4.1 0.7 %copy-done.2 = s32[16,15]{1,0:T(8,128)S(1)} copy-done((s32[16,15]{1,0:T(8,128)S(1)}, s32[16,15]{1,0:T(8,128)}, u32[]{:S(2)}) %copy-start.2) | copy-done | bytes 984
  4.8 0.0 copy-start.3
  4.8 0.7 %copy-done.3 = s32[16,3]{0,1:T(4,128)S(1)} copy-done((s32[16,3]{0,1:T(4,128)S(1)}, s32[16,3]{0,1:T(4,128)}, u32[]{:S(2)}) %copy-start.3) | copy-done | bytes 216
  5.5 33.7 %shard_map.46 = f32[2,7,4,64]{3,2,1,0:T(4,128)S(1)} custom-call(s32[3,16]{1,0:T(4,128)S(1)} %bitcast.5, s32[16,15]{1,0:T(8,128)S(1)} %copy-done.2, f32[16,3,4,64]{3,2,1,0:T(4,128)S(1)} %bitcast.4, f32[16,15,64,64]{3,2,1,0:T(8,128)S(1)} %copy-done), custom_call_target="tpu_custom_call" | custom-call | tf_op jit(solution)/shard_map/pallas_call | solution.py:399
  39.2 0.6 %copy.6 = f32[2,7,64,4]{2,3,1,0:T(4,128)} copy(f32[2,7,64,4]{2,3,1,0:T(4,128)S(1)} %bitcast.3) | data formatting | bytes 28672
Async XLA Ops:
  0.0 3.2 %copy-start = (f32[16,15,64,64]{3,2,1,0:T(8,128)S(1)}, f32[16,15,64,64]{3,2,1,0:T(8,128)}, u32[]{:S(2)}) copy-start(f32[16,15,64,64]{3,2,1,0:T(8,128)} %k_hbm.1) | copy-start | bytes 11796484
  3.2 0.9 %copy-start.1 = (f32[16,3,64,4]{2,3,1,0:T(4,128)S(1)}, f32[16,3,64,4]{2,3,1,0:T(4,128)}, u32[]{:S(2)}) copy-start(f32[16,3,64,4]{2,3,1,0:T(4,128)} %param.6) | copy-start | bytes 147460
  4.1 0.7 %copy-start.2 = (s32[16,15]{1,0:T(8,128)S(1)}, s32[16,15]{1,0:T(8,128)}, u32[]{:S(2)}) copy-start(s32[16,15]{1,0:T(8,128)} %k_cols.1) | copy-start | bytes 2884
  4.8 0.7 %copy-start.3 = (s32[16,3]{0,1:T(4,128)S(1)}, s32[16,3]{0,1:T(4,128)}, u32[]{:S(2)}) copy-start(s32[16,3]{0,1:T(4,128)} %param.7) | copy-start | bytes 580

commit v2 on v1

--- a/solution.py
+++ b/solution.py
@@ -9,6 +9,9 @@
 
 AGG = 8
 RING = 8
+PIECES = 2
+REACH = (1, -1, 2, -2)
+SENDS = 64
 MESH = pl.DeviceIdType.MESH
 F32 = jnp.float32
 BF16 = jnp.bfloat16
@@ -16,11 +19,13 @@
 
 def kernel(
     row_count,
-    p_cols,
-    k_cols,
+    p_cols_hbm,
+    k_cols_hbm,
     p_hbm,
     k_hbm,
     out,
+    p_cols,
+    k_cols,
     p_buf,
     k_buf,
     k_split,
@@ -37,6 +42,7 @@
     side_in,
     final,
     p_sem,
+    cols_sem,
     k_sem,
     ring_send,
     ring_recv,
@@ -50,18 +56,26 @@
     col = lax.axis_index("col")
     z = lax.div(col, 2)
     core = lax.rem(col, 2)
-    right = (row, lax.rem(z + 1, RING) * 2 + core)
-    left = (row, lax.rem(z + RING - 1, RING) * 2 + core)
+
+    def along(places):
+        return (row, lax.rem(z + places % RING, RING) * 2 + core)
+
     twin = (row, z * 2 + 1 - core)
     above = [(lax.rem(row + 1, row_count), z * 2 + n) for n in range(2)]
     below = [(lax.rem(row + row_count - 1, row_count), z * 2 + n) for n in range(2)]
-    peers = [right, left, twin] + above + below
-
+    peers = [along(places) for places in REACH] + [twin] + above + below
+
+    p_copy = pltpu.make_async_copy(p_hbm, p_buf, p_sem)
+    p_copy.start()
+    cols_copies = [
+        pltpu.make_async_copy(p_cols_hbm, p_cols, cols_sem.at[0]),
+        pltpu.make_async_copy(k_cols_hbm, k_cols, cols_sem.at[1]),
+    ]
+    for copy in cols_copies:
+        copy.start()
     barrier = pltpu.get_barrier_semaphore()
     for peer in peers:
         pl.semaphore_signal(barrier, inc=1, device_id=peer, device_id_type=MESH)
-    p_copy = pltpu.make_async_copy(p_hbm, p_buf, p_sem)
-    p_copy.start()
     k_copies = []
     for part in range(4):
         rows = pl.ds(4 * part, 4)
@@ -81,6 +95,7 @@
     def swap_lanes(value):
         return pltpu.roll(value, 64, 1)
 
+    cols_copies[0].wait()
     p_copy.wait()
 
     def window(j, u):
@@ -108,38 +123,39 @@
 
     pl.semaphore_wait(barrier, len(peers))
 
-    def ring_copy(way, step, half):
-        part = pl.ds(6 * half, 6)
-        slot = 7 - step if way == 0 else 1 + step
-        before = slot + 1 if way == 0 else slot - 1
-        source = chunk.at[core, part] if step == 0 else ring.at[before, part]
+    started = []
+    width = 12 // PIECES
+
+    def ring_copy(slot, places, piece, index):
+        part = pl.ds(width * piece, width)
+        source = chunk.at[core, part] if slot == 0 else ring.at[slot, part]
+        target = (slot - places) % RING
         return pltpu.make_async_remote_copy(
             src_ref=source,
-            dst_ref=ring.at[slot, part],
-            send_sem=ring_send.at[way, step, half],
-            recv_sem=ring_recv.at[way, step, half],
-            device_id=right if way == 0 else left,
+            dst_ref=ring.at[target, part],
+            send_sem=ring_send.at[index],
+            recv_sem=ring_recv.at[target, piece],
+            device_id=along(places),
             device_id_type=MESH,
         )
 
-    started = []
-    ring_copies = {}
-
-    def send_ring(step, half):
-        for way in range(2):
-            if step < 3 or way == half:
-                copy = ring_copy(way, step, half)
-                copy.start()
-                started.append(copy)
-                ring_copies[way, step, half] = copy
-
-    def take_ring(step, half):
-        for way in range(2):
-            if step < 3 or way == half:
-                ring_copies[way, step, half].wait_recv()
-
-    for half in range(2):
-        send_ring(0, half)
+    def send(slot, places, piece):
+        copy = ring_copy(slot, places, piece, len(ring_started))
+        copy.start()
+        started.append(copy)
+        ring_started.append(copy)
+
+    ring_started = []
+
+    def take(slot, piece):
+        ring_copy((slot + 1) % RING, 1, piece, 0).wait_recv()
+
+    for piece in range(PIECES):
+        send(0, 2, piece)
+        send(0, -2, piece)
+    for piece in range(PIECES):
+        send(0, 1, piece)
+        send(0, -1, piece)
     pair_copy = pltpu.make_async_remote_copy(
         src_ref=chunk.at[core],
         dst_ref=chunk.at[core],
@@ -184,10 +200,15 @@
 
     split_part(0)
     split_part(1)
-    take_ring(0, 0)
-    send_ring(1, 0)
-    take_ring(0, 1)
-    send_ring(1, 1)
+    for piece in range(PIECES):
+        take(6, piece)
+        if piece < PIECES // 2:
+            send(6, 2, piece)
+        send(6, 1, piece)
+        take(2, piece)
+        if piece >= PIECES // 2:
+            send(2, -2, piece)
+        send(2, -1, piece)
     split_part(2)
     split_part(3)
 
@@ -229,10 +250,9 @@
         return carry
 
     lax.fori_loop(0, 2, place_halo, 0)
-    take_ring(1, 0)
-    send_ring(2, 0)
-    take_ring(1, 1)
-    send_ring(2, 1)
+    pass
+
+    cols_copies[1].wait()
 
     def entry(i, s):
         if s >= 15:
@@ -281,10 +301,9 @@
         return carry
 
     lax.fori_loop(0, 4, multiply, 0)
-    take_ring(2, 0)
-    send_ring(3, 0)
-    take_ring(2, 1)
-    send_ring(3, 1)
+    for piece in range(PIECES):
+        take(7, piece)
+        take(1, piece)
     lax.fori_loop(4, 8, multiply, 0)
 
     order = (0, 1, 7, 2, 6, 3, 5, 4)
@@ -323,11 +342,11 @@
     for n in range(5):
         prepare(n, order[n])
     products(0, 5)
-    for n in range(5, 7):
+    for piece in range(PIECES):
+        for slot in (3, 5, 4):
+            take(slot, piece)
+    for n in range(5, 8):
         prepare(n, order[n])
-    take_ring(3, 0)
-    take_ring(3, 1)
-    prepare(7, order[7])
     products(5, 3)
 
     def packed(kind, t):
@@ -364,10 +383,7 @@
         device_id_type=MESH,
     )
     twin_copy.start()
-    for copy in started:
-        copy.wait_send()
-    pair_copy.wait_send()
-    twin_copy.wait()
+    twin_copy.wait_recv()
     for way in range(2):
         for n in range(2):
             side_copy(way, n, n).wait_recv()
@@ -391,6 +407,8 @@
         for band in range(7):
             a = 64 * block + 8 * band
             out[block, band] = jnp.where(even_core, turned[a : a + 4], turned[a + 4 : a + 8])
+    for copy in started + [pair_copy, twin_copy]:
+        copy.wait_send()
 
 
 def body(row_count, k_vals, k_cols, p_vals, p_cols):
@@ -400,13 +418,15 @@
         functools.partial(kernel, row_count),
         out_shape=jax.ShapeDtypeStruct((2, 7, 4, 64), F32),
         in_specs=[
-            pl.BlockSpec(memory_space=pltpu.SMEM),
-            pl.BlockSpec(memory_space=pltpu.SMEM),
+            pl.BlockSpec(memory_space=pl.ANY),
+            pl.BlockSpec(memory_space=pl.ANY),
             pl.BlockSpec(memory_space=pl.ANY),
             pl.BlockSpec(memory_space=pl.ANY),
         ],
         out_specs=pl.BlockSpec(memory_space=pltpu.VMEM),
         scratch_shapes=[
+            pltpu.SMEM((3, own), jnp.int32),
+            pltpu.SMEM((own, 15), jnp.int32),
             pltpu.VMEM((own, 3, 4, 64), F32),
             pltpu.VMEM((own, 15, 64, 64), F32),
             pltpu.VMEM((own, 4, 128, 256), BF16),
@@ -423,9 +443,10 @@
             pltpu.VMEM((2, 2, 2, 8, 128), F32),
             pltpu.VMEM((RING, 8, 128), F32),
             dma,
+            dma((2,)),
             dma((4,)),
-            dma((2, 4, 2)),
-            dma((2, 4, 2)),
+            dma((SENDS,)),
+            dma((RING, PIECES)),
             dma((4,)),
             dma((2, 2)),
             dma((2, 2)),
@@ -433,7 +454,7 @@
             dma((2, 2)),
         ],
         compiler_params=pltpu.CompilerParams(
-            collective_id=0, has_side_effects=True, vmem_limit_bytes=40 * 1024 * 1024
+            collective_id=0, has_side_effects=True, vmem_limit_bytes=62 * 1024 * 1024
         ),
     )(jnp.transpose(p_cols), k_cols, jnp.transpose(p_vals, (0, 1, 3, 2)), k_vals)
     return jnp.transpose(result, (0, 1, 3, 2))

time: 40 us -> 31.6 us (0.79)
  local copies, waits for them, and re-layouts: 6.11 us -> 1.36 us
  Pallas kernels: 33.7 us -> 30 us
    unnamed x9 -> x1, local copies, waits for them, and re-layouts: 6.11 us -> 1.36 us
    pallas_call x1, Pallas kernels: 33.7 us -> 30 us  [body(): pl.pallas_call(functools.partial(kernel, row_count), out_shape=jax.ShapeD...]
where the time goes in v2:
time: 31.6 us; the launch traced here: 31.4 us
  Pallas kernels  30 us (95%)
  local copies, waits for them, and re-layouts  1.36 us (4%)
    pallas_call x1, Pallas kernels, body(): pl.pallas_call(functools.partial(kernel, row_count), out_shape=jax.ShapeD...  30 us
    unnamed x1, local copies, waits for them, and re-layouts  1.36 us

profile of v2, /device:TPU:1, one launch (start us, length us, event | category | flops | bytes accessed | tf_op | source)
XLA Modules:
  0.0 31.4 jit_solution(4217318453399937583)
XLA Ops:
  0.0 30.0 %shard_map.46 = f32[2,7,4,64]{3,2,1,0:T(4,128)} custom-call(s32[3,16]{1,0:T(4,128)} %bitcast.5, s32[16,15]{1,0:T(8,128)} %k_cols_hbm.1, f32[16,3,4,64]{3,2,1,0:T(4,128)} %bitcast.4, f32[16,15,64,64]{3,2,1,0:T(8,128)} %k_hbm.1), custom_call_target="tpu_custom_call" | custom-call | tf_op jit(solution)/shard_map/pallas_call | solution.py:417
  30.0 1.4 %copy.6 = f32[2,7,64,4]{2,3,1,0:T(4,128)} copy(f32[2,7,64,4]{2,3,1,0:T(4,128)} %bitcast.3) | data formatting | bytes 28672

commit v3 on v2

v3 whole, which is shorter than its diff:
```python
import functools

import jax
import jax.numpy as jnp
from jax import lax
from jax.experimental import pallas as pl
from jax.experimental.pallas import tpu as pltpu
from jax.sharding import PartitionSpec as P

AGG = 8
RING = 8
REACH = (2, -2, 1, -1)
MESH = pl.DeviceIdType.MESH
F32 = jnp.float32
BF16 = jnp.bfloat16


def kernel(
    row_count,
    p_cols_hbm,
    k_cols_hbm,
    p_hbm,
    k_hbm,
    out,
    p_cols,
    k_cols,
    p_buf,
    k_buf,
    k_split,
    near,
    ring,
    table,
    weights,
    left_side,
    terms,
    packed,
    twin_in,
    side_in,
    final,
    local_sem,
    ring_send,
    ring_recv,
    pair_sem,
    halo_send,
    halo_recv,
    side_send,
    side_recv,
):
    row = lax.axis_index("row")
    col = lax.axis_index("col")
    z = lax.div(col, 2)
    core = lax.rem(col, 2)
    own_rows = 2 * AGG
    first_row = row * own_rows
    total_rows = row_count * own_rows
    blocks_all = total_rows // AGG
    has_above = row < row_count - 1
    has_below = row > 0
    lower = core == 0
    has_side = jnp.where(lower, row, row_count - 1 - row) > 0
    has_other = jnp.where(lower, row_count - 1 - row, row) > 0
    side_row = row - 1 + 2 * core
    other_row = row + 1 - 2 * core
    twin = (row, z * 2 + 1 - core)

    def along(places, which):
        return (row, lax.rem(z + places % RING, RING) * 2 + which)

    copies = [
        pltpu.make_async_copy(p_hbm, p_buf, local_sem.at[0]),
        pltpu.make_async_copy(p_cols_hbm, p_cols, local_sem.at[1]),
        pltpu.make_async_copy(k_cols_hbm, k_cols, local_sem.at[2]),
    ]
    for copy in copies:
        copy.start()
    barrier = pltpu.get_barrier_semaphore()

    def greet(peer):
        pl.semaphore_signal(barrier, inc=1, device_id=peer, device_id_type=MESH)

    greet(twin)
    for places in REACH:
        for which in range(2):
            greet(along(places, which))

    @pl.when(has_side)
    def _():
        for which in range(2):
            greet((side_row, z * 2 + which))

    @pl.when(has_other)
    def _():
        greet((other_row, z * 2 + core))

    k_copies = []
    for part in range(2):
        k_copies.append(
            pltpu.make_async_copy(
                k_hbm.at[pl.ds(AGG * core + 4 * part, 4)], k_buf.at[pl.ds(4 * part, 4)], local_sem.at[3 + part]
            )
        )
        k_copies[-1].start()

    top = lax.broadcasted_iota(jnp.int32, (8, 128), 0) < 4
    low = lax.broadcasted_iota(jnp.int32, (8, 128), 1) < 64

    def swap_rows(value):
        return pltpu.roll(value, 4, 0)

    def swap_lanes(value):
        return pltpu.roll(value, 64, 1)

    copies[1].wait()
    copies[0].wait()

    def window(j, u):
        total = jnp.zeros((4, 64), F32)
        for t in range(3):
            block = p_cols[t, j]
            position = block - (2 * row + j // AGG) + 1
            position = jnp.where((block >= 0) & (block < blocks_all), position, -1)
            total = total + jnp.where(jnp.full((4, 64), position) == u, p_buf[j, t], 0.0)
        return total

    for h in range(2):
        for m in range(2):
            for u in range(3):
                halves = []
                for x in range(2):
                    j = AGG * h + 4 * m + 2 * x
                    halves.append(jnp.concatenate([window(j, u), window(j + 1, u)], axis=1))
                near[h + 1 - core, core, m * 3 + u] = jnp.concatenate(halves, axis=0)

    @pl.when(jnp.logical_not(has_side))
    def _():
        near[2 * core] = jnp.zeros((2, 6, 8, 128), F32)

    @pl.when(jnp.logical_not(has_below))
    def _():
        side_in[0] = jnp.zeros((4, 8, 128), F32)

    @pl.when(jnp.logical_not(has_above))
    def _():
        side_in[1] = jnp.zeros((4, 8, 128), F32)

    greeted = jnp.where(has_side, 2, 0) + jnp.where(has_other, 1, 0) + 2 * len(REACH) + 1
    pl.semaphore_wait(barrier, greeted)

    started = []

    def ring_copy(source, slot, places, which, part, index):
        target = (slot - places) % RING
        return pltpu.make_async_remote_copy(
            src_ref=source,
            dst_ref=ring.at[target, part],
            send_sem=ring_send.at[index],
            recv_sem=ring_recv.at[target, part],
            device_id=along(places, which),
            device_id_type=MESH,
        )

    def begin(*arguments):
        copy = ring_copy(*arguments, len(started))
        copy.start()
        started.append(copy)

    def take(slot, part):
        ring_copy(ring.at[slot, part], (slot + 1) % RING, 1, core, part, 0).wait_recv()

    for places in REACH:
        for h in range(2):
            begin(near.at[h + 1 - core, core], 0, places, h, core)

    pair_copy = pltpu.make_async_remote_copy(
        src_ref=near.at[pl.ds(1 - core, 2), core],
        dst_ref=near.at[pl.ds(core, 2), core],
        send_sem=pair_sem.at[0],
        recv_sem=pair_sem.at[1],
        device_id=twin,
        device_id_type=MESH,
    )
    pair_copy.start()
    pair_take = pltpu.make_async_remote_copy(
        src_ref=near.at[pl.ds(core, 2), 1 - core],
        dst_ref=near.at[pl.ds(1 - core, 2), 1 - core],
        send_sem=pair_sem.at[0],
        recv_sem=pair_sem.at[1],
        device_id=twin,
        device_id_type=MESH,
    )

    def halo_copy(h):
        return pltpu.make_async_remote_copy(
            src_ref=near.at[h + 1 - core, core],
            dst_ref=near.at[2 - 2 * h, core],
            send_sem=halo_send.at[h],
            recv_sem=halo_recv.at[core],
            device_id=(row - 1 + 2 * h, z * 2 + 1 - h),
            device_id_type=MESH,
        )

    def halo_take(sender):
        pltpu.make_async_remote_copy(
            src_ref=near.at[1, sender],
            dst_ref=near.at[2 * core, sender],
            send_sem=halo_send.at[0],
            recv_sem=halo_recv.at[sender],
            device_id=(side_row, z * 2 + sender),
            device_id_type=MESH,
        ).wait_recv()

    @pl.when(has_below)
    def _():
        halo_copy(0).start()

    @pl.when(has_above)
    def _():
        halo_copy(1).start()

    def split_k(i, carry):
        for q in range(4):
            pairs = []
            for s in (4 * q, 4 * q + 2):
                second = k_buf[i, s + 1] if s + 1 < 15 else jnp.zeros((64, 64), F32)
                pairs.append(jnp.concatenate([k_buf[i, s], second], axis=1))
            both = jnp.concatenate(pairs, axis=1)
            high = both.astype(BF16)
            k_split[i, q, 0:64] = high
            k_split[i, q, 64:128] = (both - high.astype(F32)).astype(BF16)
        return carry

    def split_part(part):
        k_copies[part].wait()
        lax.fori_loop(4 * part, 4 * part + 4, split_k, 0)

    def merge(zero, one):
        mixed = swap_rows(jnp.where(top, one, zero))
        return jnp.where(top, zero, mixed), jnp.where(top, mixed, one)

    def place_group(side):
        def place(m, carry):
            merged = [merge(near[side, 0, m * 3 + u], near[side, 1, m * 3 + u]) for u in range(3)]
            for x in range(2):
                for flipped in range(2):
                    blocks = [swap_lanes(merged[u][x]) if flipped else merged[u][x] for u in range(3)]
                    if side > 0:
                        blocks = [jnp.zeros((8 * side, 128), F32)] + blocks
                    whole = jnp.concatenate(blocks + [jnp.zeros((8 * (3 - side), 128), F32)], axis=0)
                    high = whole.astype(BF16)
                    entry_at = 8 * side + 4 * m + 2 * x + flipped
                    table[entry_at, 0] = high
                    table[entry_at, 1] = (whole - high.astype(F32)).astype(BF16)
            return carry

        lax.fori_loop(0, 2, place, 0)

    split_part(0)
    split_part(1)
    pair_take.wait_recv()
    table[24:26] = jnp.zeros((2, 2, 48, 128), BF16)
    place_group(1)
    for part in range(2):
        take(6, part)
        begin(ring.at[6, part], 6, 1, core, part)
        if part == 0:
            begin(ring.at[6, part], 6, 2, core, part)
        take(2, part)
        begin(ring.at[2, part], 2, -1, core, part)
        if part == 1:
            begin(ring.at[2, part], 2, -2, core, part)

    @pl.when(has_side)
    def _():
        for sender in range(2):
            halo_take(sender)

    place_group(0)
    place_group(2)
    copies[2].wait()

    def entry(i, s):
        if s >= 15:
            return 24
        block = k_cols[AGG * core + i, s]
        place_of = block - (first_row + AGG * core - AGG)
        inside = (block >= 0) & (block < total_rows) & (place_of >= 0) & (place_of < 24)
        return jnp.where(inside, place_of, 24)

    low_16 = lax.broadcasted_iota(jnp.int32, (48, 128), 1) < 64
    low_64 = lax.broadcasted_iota(jnp.int32, (64, 128), 1) < 64
    blank = jnp.zeros((16, 128), BF16)

    def multiply_row(i, swapped):
        total = None
        for q in range(4):
            sides = []
            for s in (4 * q, 4 * q + 2):
                even = entry(i, s)
                odd = lax.bitwise_xor(entry(i, s + 1), 1)
                parts = [jnp.where(low_16, table[even, part], table[odd, part]) for part in range(2)]
                if swapped:
                    parts = parts[::-1]
                sides.append(jnp.concatenate([parts[0], blank, parts[1], blank], axis=0))
            term = lax.dot_general(
                k_split[i, q],
                jnp.concatenate(sides, axis=1),
                (((1,), (1,)), ((), ())),
                preferred_element_type=F32,
            )
            total = term if total is None else total + term
        return total[0:64], total[64:128]

    def multiply(n, carry):
        i = n + 2 * (n // 2)
        a_0, b_0 = multiply_row(i, False)
        a_1, b_1 = multiply_row(i + 2, True)
        value = jnp.where(low_64, a_0 + b_0, a_1 + b_1)
        value = value + swap_lanes(jnp.where(low_64, a_1, a_0))
        high = value.astype(BF16)
        rows = pl.ds(pl.multiple_of(64 * n, 64), 64)
        weights[rows, 0:128] = high
        weights[rows, 128:256] = (value - high.astype(F32)).astype(BF16)
        return carry

    lax.fori_loop(0, 4, multiply, 0)

    def prepare(place_at, slot):
        for part in range(2):

            def tile(m, u):
                return near[1, part, m * 3 + u] if slot == 0 else ring[slot, part, m * 3 + u]

            whole = jnp.concatenate(
                [jnp.concatenate([tile(m, u) for m in range(2)], axis=1) for u in range(3)], axis=0
            )
            rest = whole - whole.astype(BF16).astype(F32)
            rows = pl.ds(96 * place_at + 48 * part, 48)
            left_side[rows] = jnp.concatenate([whole, rest], axis=0).astype(BF16)

    def products(first, slots):
        count = len(slots)
        result = lax.dot_general(
            left_side[pl.ds(96 * first, 96 * count)],
            weights[...],
            (((1,), (0,)), ((), ())),
            preferred_element_type=F32,
        )
        for n, slot in enumerate(slots):
            for u in range(3):
                folded = []
                for part in range(2):
                    a = 96 * n + 48 * part + 8 * u
                    value = result[a : a + 8, 0:128] + result[a : a + 8, 128:256]
                    value = value + result[a + 24 : a + 32, 0:128]
                    folded.append(jnp.where(top, value, swap_lanes(value)))
                value = jnp.where(top, folded[0], folded[1])
                value = value + swap_rows(jnp.where(top, folded[1], folded[0]))
                terms[u, slot] = value if u == 2 else pltpu.roll(value, 16 - 8 * u, 1)

    early, late = (0, 2, 6, 1, 7), (3, 5, 4)
    for part in range(2):
        take(7, part)
        take(1, part)
    for n, slot in enumerate(early):
        prepare(n, slot)
    products(0, early)
    for n, slot in enumerate(late):
        for part in range(2):
            take(slot, part)
        prepare(5 + n, slot)
    products(5, late)

    for u in range(3):
        for t in range(4):
            packed[u, t] = jnp.where(low, terms[u, t], swap_lanes(terms[u, t + 4]))

    def side_copy(n):
        return pltpu.make_async_remote_copy(
            src_ref=packed.at[2 * core],
            dst_ref=side_in.at[1 - core],
            send_sem=side_send.at[n],
            recv_sem=side_recv.at[1 - core],
            device_id=(side_row, z * 2 + n),
            device_id_type=MESH,
        )

    def side_take(n):
        pltpu.make_async_remote_copy(
            src_ref=packed.at[0],
            dst_ref=side_in.at[n],
            send_sem=side_send.at[0],
            recv_sem=side_recv.at[n],
            device_id=(row - 1 + 2 * n, z * 2 + 1 - n),
            device_id_type=MESH,
        ).wait_recv()

    @pl.when(has_side)
    def _():
        for n in range(2):
            side_copy(n).start()

    twin_copy = pltpu.make_async_remote_copy(
        src_ref=packed.at[pl.ds(1 - core, 2)],
        dst_ref=twin_in,
        send_sem=pair_sem.at[2],
        recv_sem=pair_sem.at[3],
        device_id=twin,
        device_id_type=MESH,
    )
    twin_copy.start()
    twin_copy.wait_recv()

    @pl.when(has_below)
    def _():
        side_take(0)

    @pl.when(has_above)
    def _():
        side_take(1)

    for t in range(4):
        first, second = [packed[n + 1 - core, t] + twin_in[n, t] + side_in[n, t] for n in range(2)]
        final[lax.rem(z + t, RING)] = jnp.where(low, first, swap_lanes(second))
        final[lax.rem(z + t + 4, RING)] = jnp.where(low, swap_lanes(first), second)
    turned = jnp.transpose(jnp.concatenate([final[n] for n in range(RING)], axis=0))
    even_core = jnp.full((4, 64), core) == 0
    for block in range(2):
        for band in range(7):
            a = 64 * block + 8 * band
            out[block, band] = jnp.where(even_core, turned[a : a + 4], turned[a + 4 : a + 8])

    for copy in started + [pair_copy, twin_copy]:
        copy.wait_send()

    @pl.when(has_below)
    def _():
        halo_copy(0).wait_send()

    @pl.when(has_above)
    def _():
        halo_copy(1).wait_send()

    @pl.when(has_side)
    def _():
        for n in range(2):
            side_copy(n).wait_send()


def body(row_count, k_vals, k_cols, p_vals, p_cols):
    own = k_vals.shape[0]
    dma = pltpu.SemaphoreType.DMA
    operands = [jnp.transpose(p_cols), k_cols, jnp.transpose(p_vals, (0, 1, 3, 2)), k_vals]
    result = pl.pallas_call(
        functools.partial(kernel, row_count),
        out_shape=jax.ShapeDtypeStruct((2, 7, 4, 64), F32),
        in_specs=[pl.BlockSpec(memory_space=pltpu.HBM)] * 4,
        out_specs=pl.BlockSpec(memory_space=pltpu.VMEM),
        scratch_shapes=[
            pltpu.SMEM((3, own), jnp.int32),
            pltpu.SMEM((own, 15), jnp.int32),
            pltpu.VMEM((own, 3, 4, 64), F32),
            pltpu.VMEM((AGG, 15, 64, 64), F32),
            pltpu.VMEM((AGG, 4, 128, 256), BF16),
            pltpu.VMEM((3, 2, 6, 8, 128), F32),
            pltpu.VMEM((RING, 2, 6, 8, 128), F32),
            pltpu.VMEM((26, 2, 48, 128), BF16),
            pltpu.VMEM((256, 256), BF16),
            pltpu.VMEM((768, 256), BF16),
            pltpu.VMEM((3, RING, 8, 128), F32),
            pltpu.VMEM((3, 4, 8, 128), F32),
            pltpu.VMEM((2, 4, 8, 128), F32),
            pltpu.VMEM((2, 4, 8, 128), F32),
            pltpu.VMEM((RING, 8, 128), F32),
            dma((5,)),
            dma((16,)),
            dma((RING, 2)),
            dma((4,)),
            dma((2,)),
            dma((2,)),
            dma((2,)),
            dma((2,)),
        ],
        compiler_params=pltpu.CompilerParams(
            collective_id=0, has_side_effects=True, vmem_limit_bytes=32 * 1024 * 1024
        ),
    )(*[pltpu.with_memory_space_constraint(operand, pltpu.HBM) for operand in operands])
    return jnp.transpose(result, (0, 1, 3, 2))


def solution(mesh):
    placed = (
        P("row", None, None, None),
        P("row", None),
        P("row", None, None, "col"),
        P("row", None),
    )
    return jax.shard_map(
        functools.partial(body, mesh.shape["row"]),
        mesh=mesh,
        in_specs=placed,
        out_specs=P("row", None, None, "col"),
        check_vma=False,
    )
```

time: 31.6 us -> 25.8 us (0.82)
  the two profiles are of different devices: /device:TPU:1 before, /device:TPU:7 now
where the time goes in v3:
time: 25.8 us; the launch traced here: 25.6 us
  Pallas kernels  25 us (97%)
  local copies, waits for them, and re-layouts  0.61 us (2%)
    pallas_call x1, Pallas kernels, body(): pl.pallas_call(functools.partial(kernel, row_count), out_shape=jax.ShapeD...  25 us
    unnamed x1, local copies, waits for them, and re-layouts  0.61 us

profile of v3, /device:TPU:7, one launch (start us, length us, event | category | flops | bytes accessed | tf_op | source)
XLA Modules:
  0.0 25.6 jit_solution(15212229655950177751)
XLA Ops:
  0.0 25.0 %shard_map.46 = f32[2,7,4,64]{3,2,1,0:T(4,128)S(1)} custom-call(s32[3,16]{1,0:T(4,128)} %bitcast.5, s32[16,15]{1,0:T(8,128)} %k_cols_hbm.1, f32[16,3,4,64]{3,2,1,0:T(4,128)} %bitcast.4, f32[16,15,64,64]{3,2,1,0:T(8,128)} %k_hbm.1), custom_call_target="tpu_custom_call" | custom-call | tf_op jit(solution)/shard_map/pallas_call | solution.py:453
  25.0 0.6 %copy.6 = f32[2,7,64,4]{2,3,1,0:T(4,128)} copy(f32[2,7,64,4]{2,3,1,0:T(4,128)S(1)} %bitcast.3) | data formatting | bytes 28672

commit v4 on v3

v4 whole, which is shorter than its diff:
```python
import functools

import jax
import jax.numpy as jnp
from jax import lax
from jax.experimental import pallas as pl
from jax.experimental.pallas import tpu as pltpu
from jax.sharding import PartitionSpec as P

AGG = 8
RING = 8
SPREAD = ((3, -3), (2, 2), (1, -1))
MESH = pl.DeviceIdType.MESH
F32 = jnp.float32
BF16 = jnp.bfloat16


def kernel(
    row_count,
    p_cols_hbm,
    k_cols_hbm,
    p_hbm,
    k_hbm,
    out,
    p_cols,
    k_cols,
    p_buf,
    k_buf,
    k_split,
    near,
    ring,
    table,
    weights,
    left_side,
    terms,
    packed,
    pair_in,
    side_in,
    final,
    local_sem,
    ring_send,
    ring_recv,
    pair_send,
    pair_recv,
    last_recv,
    halo_send,
    halo_recv,
    side_send,
    side_recv,
):
    row = lax.axis_index("row")
    col = lax.axis_index("col")
    z = lax.div(col, 2)
    core = lax.rem(col, 2)
    own_rows = 2 * AGG
    first_row = row * own_rows
    total_rows = row_count * own_rows
    blocks_all = total_rows // AGG
    has_above = row < row_count - 1
    has_below = row > 0
    lower = core == 0
    has_side = jnp.where(lower, row, row_count - 1 - row) > 0
    has_other = jnp.where(lower, row_count - 1 - row, row) > 0
    side_row = row - 1 + 2 * core
    other_row = row + 1 - 2 * core
    odd = lax.rem(z, 2)
    turn = 1 - 2 * odd
    me = odd * 2 + core

    def along(places, which):
        return (row, lax.rem(z + turn * places + RING, RING) * 2 + which)

    def member(at_row, number):
        return (at_row, (z - odd) * 2 + number)

    pair_peers = [(row, z * 2 + 1 - core), along(1, 0), along(1, 1)]

    copies = [
        pltpu.make_async_copy(p_hbm, p_buf, local_sem.at[0]),
        pltpu.make_async_copy(p_cols_hbm, p_cols, local_sem.at[1]),
        pltpu.make_async_copy(k_cols_hbm, k_cols, local_sem.at[2]),
    ]
    for copy in copies:
        copy.start()
    barrier = pltpu.get_barrier_semaphore()

    def greet(peer):
        pl.semaphore_signal(barrier, inc=1, device_id=peer, device_id_type=MESH)

    for peer in pair_peers:
        greet(peer)
    for places in (-1, 2, -2, -3):
        for which in range(2):
            greet(along(places, which))

    @pl.when(has_side)
    def _():
        for number in range(4):
            greet(member(side_row, number))

    @pl.when(has_other)
    def _():
        for n in range(2):
            greet(member(other_row, 2 * n + core))

    k_copies = []
    for part in range(2):
        k_copies.append(
            pltpu.make_async_copy(
                k_hbm.at[pl.ds(AGG * core + 4 * part, 4)], k_buf.at[pl.ds(4 * part, 4)], local_sem.at[3 + part]
            )
        )
        k_copies[-1].start()

    top = lax.broadcasted_iota(jnp.int32, (8, 128), 0) < 4
    low = lax.broadcasted_iota(jnp.int32, (8, 128), 1) < 64

    def swap_rows(value):
        return pltpu.roll(value, 4, 0)

    def swap_lanes(value):
        return pltpu.roll(value, 64, 1)

    copies[1].wait()
    copies[0].wait()

    def window(j, u):
        total = jnp.zeros((4, 64), F32)
        for t in range(3):
            block = p_cols[t, j]
            position = block - (2 * row + j // AGG) + 1
            position = jnp.where((block >= 0) & (block < blocks_all), position, -1)
            total = total + jnp.where(jnp.full((4, 64), position) == u, p_buf[j, t], 0.0)
        return total

    for h in range(2):
        for m in range(2):
            for u in range(3):
                halves = []
                for x in range(2):
                    j = AGG * h + 4 * m + 2 * x
                    halves.append(jnp.concatenate([window(j, u), window(j + 1, u)], axis=1))
                near[h + 1 - core, me, m * 3 + u] = jnp.concatenate(halves, axis=0)

    @pl.when(jnp.logical_not(has_side))
    def _():
        near[2 * core] = jnp.zeros((4, 6, 8, 128), F32)

    @pl.when(jnp.logical_not(has_below))
    def _():
        for n in range(2):
            side_in[n, 0] = jnp.zeros((8, 128), F32)

    @pl.when(jnp.logical_not(has_above))
    def _():
        for n in range(2):
            side_in[n, 1] = jnp.zeros((8, 128), F32)

    pl.semaphore_wait(barrier, jnp.where(has_side, 4, 0) + jnp.where(has_other, 2, 0) + 11)

    def pair_copy(n, number, which, peer):
        return pltpu.make_async_remote_copy(
            src_ref=near.at[pl.ds(1 - core, 2), number],
            dst_ref=near.at[pl.ds(1 - which, 2), number],
            send_sem=pair_send.at[n],
            recv_sem=pair_recv.at[number],
            device_id=peer,
            device_id_type=MESH,
        )

    started = []
    for n, peer in enumerate(pair_peers):
        started.append(pair_copy(n, me, 1 - core if n == 0 else n - 1, peer))
        started[-1].start()

    def halo_copy(h, n):
        return pltpu.make_async_remote_copy(
            src_ref=near.at[h + 1 - core, me],
            dst_ref=near.at[2 - 2 * h, me],
            send_sem=halo_send.at[h, n],
            recv_sem=halo_recv.at[me],
            device_id=member(row - 1 + 2 * h, 2 * n + 1 - h),
            device_id_type=MESH,
        )

    def halo_take(number):
        pltpu.make_async_remote_copy(
            src_ref=near.at[1, number],
            dst_ref=near.at[2 * core, number],
            send_sem=halo_send.at[0, 0],
            recv_sem=halo_recv.at[number],
            device_id=member(side_row, number),
            device_id_type=MESH,
        ).wait_recv()

    @pl.when(has_below)
    def _():
        for n in range(2):
            halo_copy(0, n).start()

    @pl.when(has_above)
    def _():
        for n in range(2):
            halo_copy(1, n).start()

    def ring_copy(slot, places, h, part):
        return pltpu.make_async_remote_copy(
            src_ref=near.at[h + 1 - core, me],
            dst_ref=ring.at[slot - 1, part],
            send_sem=ring_send.at[slot - 1, h],
            recv_sem=ring_recv.at[slot - 1, part],
            device_id=along(places, h),
            device_id_type=MESH,
        )

    for slot, places in SPREAD:
        for h in range(2):
            started.append(ring_copy(slot, places, h, core))
            started[-1].start()

    def take(slot, part):
        ring_copy(slot, 2, 0, part).wait_recv()

    def split_k(i, carry):
        for q in range(4):
            pairs = []
            for s in (4 * q, 4 * q + 2):
                second = k_buf[i, s + 1] if s + 1 < 15 else jnp.zeros((64, 64), F32)
                pairs.append(jnp.concatenate([k_buf[i, s], second], axis=1))
            both = jnp.concatenate(pairs, axis=1)
            high = both.astype(BF16)
            k_split[i, q, 0:64] = high
            k_split[i, q, 64:128] = (both - high.astype(F32)).astype(BF16)
        return carry

    def split_part(part):
        k_copies[part].wait()
        lax.fori_loop(4 * part, 4 * part + 4, split_k, 0)

    def place_group(side):
        empty = jnp.zeros((8, 128), F32)

        def place(m, carry):
            tiles = [[near[side, n, m * 3 + u] for u in range(3)] for n in range(4)]
            turned = [[swap_rows(tile) for tile in each] for each in tiles]
            for x in range(2):
                wholes = [[], []]
                for n in range(4):
                    upper = turned[n] if x else tiles[n]
                    under = tiles[n] if x else turned[n]
                    if side == 1:
                        found = [jnp.where(top, 0.0, under[0]), jnp.where(top, upper[1], under[2])]
                    else:
                        found = [jnp.where(top, upper[0], under[1]), jnp.where(top, upper[2], 0.0)]
                    ahead, behind = [empty] * (side // 2), [empty] * (2 - side // 2)
                    wholes[0] += ahead + found + behind
                    wholes[1] += ahead + [swap_lanes(tile) for tile in found] + behind
                for flipped in range(2):
                    whole = jnp.concatenate(wholes[flipped], axis=0)
                    high = whole.astype(BF16)
                    entry_at = 8 * side + 4 * m + 2 * x + flipped
                    table[entry_at, 0] = high
                    table[entry_at, 1] = (whole - high.astype(F32)).astype(BF16)
            return carry

        lax.fori_loop(0, 2, place, 0)

    split_part(0)
    split_part(1)
    table[24:26] = jnp.zeros((2, 2, 128, 128), BF16)
    pair_copy(0, odd * 2 + 1 - core, core, pair_peers[0]).wait_recv()
    for n in range(2):
        pair_copy(0, (1 - odd) * 2 + n, core, pair_peers[0]).wait_recv()
    place_group(1)

    @pl.when(has_side)
    def _():
        for number in range(4):
            halo_take(number)

    place_group(0)
    place_group(2)
    copies[2].wait()

    def entry(i, s):
        if s >= 15:
            return 24
        block = k_cols[AGG * core + i, s]
        place_of = block - (first_row + AGG * core - AGG)
        inside = (block >= 0) & (block < total_rows) & (place_of >= 0) & (place_of < 24)
        return jnp.where(inside, place_of, 24)

    low_16 = lax.broadcasted_iota(jnp.int32, (128, 128), 1) < 64

    def multiply_row(i):
        total = None
        for q in range(4):
            sides = []
            for s in (4 * q, 4 * q + 2):
                even = entry(i, s)
                other = lax.bitwise_xor(entry(i, s + 1), 1)
                parts = [jnp.where(low_16, table[even, part], table[other, part]) for part in range(2)]
                sides.append(jnp.concatenate(parts, axis=0))
            term = lax.dot_general(
                k_split[i, q],
                jnp.concatenate(sides, axis=1),
                (((1,), (1,)), ((), ())),
                preferred_element_type=F32,
            )
            total = term if total is None else total + term
        return total[0:64, 0:128] + total[0:64, 128:256] + total[64:128, 0:128]

    def multiply(n, carry):
        i = n + 2 * (n // 2)
        rows = pl.ds(pl.multiple_of(64 * n, 64), 64)
        for x in range(2):
            value = multiply_row(i + 2 * x)
            high = value.astype(BF16)
            weights[rows, 128 * x : 128 * x + 128] = high
            weights[rows, 256 + 128 * x : 384 + 128 * x] = (value - high.astype(F32)).astype(BF16)
        return carry

    lax.fori_loop(0, 4, multiply, 0)

    def prepare(place_at, slot):
        for part in range(2):

            def tile(m, u):
                return near[1, odd * 2 + part, m * 3 + u] if slot == 0 else ring[slot - 1, part, m * 3 + u]

            whole = jnp.concatenate(
                [jnp.concatenate([tile(m, u) for m in range(2)], axis=1) for u in range(3)], axis=0
            )
            rest = whole - whole.astype(BF16).astype(F32)
            rows = pl.ds(96 * place_at + 48 * part, 48)
            left_side[rows] = jnp.concatenate([whole, rest], axis=0).astype(BF16)

    def products(first, slots):
        count = len(slots)
        result = lax.dot_general(
            left_side[pl.ds(96 * first, 96 * count)],
            weights[...],
            (((1,), (0,)), ((), ())),
            preferred_element_type=F32,
        )
        for n, slot in enumerate(slots):
            for u in range(3):
                folded = []
                for part in range(2):
                    a = 96 * n + 48 * part + 8 * u
                    value = result[a : a + 8, 0:256] + result[a : a + 8, 256:512]
                    value = value + result[a + 24 : a + 32, 0:256]
                    folded.append(jnp.where(top, value[:, 0:128], value[:, 128:256]))
                value = jnp.where(top, folded[0], folded[1])
                value = value + swap_rows(jnp.where(top, folded[1], folded[0]))
                terms[u, slot] = value if u == 2 else pltpu.roll(value, 8 - 4 * u, 1)

    early, late = (0, 1), (2, 3)
    for part in range(2):
        take(1, part)
    for n, slot in enumerate(early):
        prepare(n, slot)
    products(0, early)
    for n, slot in enumerate(late):
        for part in range(2):
            take(slot, part)
        prepare(2 + n, slot)
    products(2, late)

    lane_group = lax.broadcasted_iota(jnp.int32, (8, 128), 1) // 32

    def rotate(value, groups):
        return value if groups % 4 == 0 else pltpu.roll(value, 32 * (groups % 4), 1)

    for u in (0, 2, 1):
        parts = [terms[u, slot] for slot in range(4)]
        for number in range(4):
            moved = [rotate(parts[slot], slot - number) for slot in range(4)]
            left_half = jnp.where(lane_group == 0, moved[0], moved[1])
            right_half = jnp.where(lane_group == 2, moved[2], moved[3])
            packed[number, u] = jnp.where(low, left_half, right_half)

    def side_copy(number):
        return pltpu.make_async_remote_copy(
            src_ref=packed.at[number, 2 * core],
            dst_ref=side_in.at[odd, 1 - core],
            send_sem=side_send.at[number],
            recv_sem=side_recv.at[odd, 1 - core],
            device_id=member(side_row, number),
            device_id_type=MESH,
        )

    def side_take(n, block):
        pltpu.make_async_remote_copy(
            src_ref=packed.at[0, 0],
            dst_ref=side_in.at[n, block],
            send_sem=side_send.at[0],
            recv_sem=side_recv.at[n, block],
            device_id=member(row - 1 + 2 * block, 2 * n + 1 - block),
            device_id_type=MESH,
        ).wait_recv()

    @pl.when(has_side)
    def _():
        for number in range(4):
            side_copy(number).start()

    def last_copy(n, number, chip, which, peer):
        return pltpu.make_async_remote_copy(
            src_ref=packed.at[number, pl.ds(1 - core, 2)],
            dst_ref=pair_in.at[chip, which],
            send_sem=pair_send.at[3 + n],
            recv_sem=last_recv.at[chip, which],
            device_id=peer,
            device_id_type=MESH,
        )

    for n, peer in enumerate(pair_peers):
        number = odd * 2 + 1 - core if n == 0 else (1 - odd) * 2 + n - 1
        started.append(last_copy(n, number, odd, core, peer))
        started[-1].start()
    pair_in[odd, core] = packed[me, pl.ds(1 - core, 2)]
    last_copy(0, 0, odd, 1 - core, pair_peers[0]).wait_recv()
    for n in range(2):
        last_copy(0, 0, 1 - odd, n, pair_peers[0]).wait_recv()

    @pl.when(has_below)
    def _():
        for n in range(2):
            side_take(n, 0)

    @pl.when(has_above)
    def _():
        for n in range(2):
            side_take(n, 1)

    for chip in range(2):
        totals = [pair_in[chip, 0, n] + pair_in[chip, 1, n] + side_in[chip, n] for n in range(2)]
        for slot in range(4):
            place_at = z - odd + chip + RING + (slot if chip else -slot)
            final[lax.rem(place_at, RING)] = jnp.where(
                lane_group == 0, rotate(totals[0], -slot), rotate(totals[1], 1 - slot)
            )
    turned = jnp.transpose(jnp.concatenate([final[n] for n in range(RING)], axis=0))
    for block in range(2):
        for band in range(7):
            a = 32 * block + 4 * band
            out[block, band] = turned[a : a + 4]

    for copy in started:
        copy.wait_send()

    @pl.when(has_below)
    def _():
        for n in range(2):
            halo_copy(0, n).wait_send()

    @pl.when(has_above)
    def _():
        for n in range(2):
            halo_copy(1, n).wait_send()

    @pl.when(has_side)
    def _():
        for number in range(4):
            side_copy(number).wait_send()


def body(row_count, k_vals, k_cols, p_vals, p_cols):
    own = k_vals.shape[0]
    dma = pltpu.SemaphoreType.DMA
    operands = [jnp.transpose(p_cols), k_cols, jnp.transpose(p_vals, (0, 1, 3, 2)), k_vals]
    result = pl.pallas_call(
        functools.partial(kernel, row_count),
        out_shape=jax.ShapeDtypeStruct((2, 7, 4, 64), F32),
        in_specs=[pl.BlockSpec(memory_space=pltpu.HBM)] * 4,
        out_specs=pl.BlockSpec(memory_space=pltpu.VMEM),
        scratch_shapes=[
            pltpu.SMEM((3, own), jnp.int32),
            pltpu.SMEM((own, 15), jnp.int32),
            pltpu.VMEM((own, 3, 4, 64), F32),
            pltpu.VMEM((AGG, 15, 64, 64), F32),
            pltpu.VMEM((AGG, 4, 128, 256), BF16),
            pltpu.VMEM((3, 4, 6, 8, 128), F32),
            pltpu.VMEM((3, 2, 6, 8, 128), F32),
            pltpu.VMEM((26, 2, 128, 128), BF16),
            pltpu.VMEM((256, 512), BF16),
            pltpu.VMEM((384, 256), BF16),
            pltpu.VMEM((3, 4, 8, 128), F32),
            pltpu.VMEM((4, 3, 8, 128), F32),
            pltpu.VMEM((2, 2, 2, 8, 128), F32),
            pltpu.VMEM((2, 2, 8, 128), F32),
            pltpu.VMEM((RING, 8, 128), F32),
            dma((5,)),
            dma((3, 2)),
            dma((3, 2)),
            dma((6,)),
            dma((4,)),
            dma((2, 2)),
            dma((2, 2)),
            dma((4,)),
            dma((4,)),
            dma((2, 2)),
        ],
        compiler_params=pltpu.CompilerParams(
            collective_id=0, has_side_effects=True, vmem_limit_bytes=32 * 1024 * 1024
        ),
    )(*[pltpu.with_memory_space_constraint(operand, pltpu.HBM) for operand in operands])
    return jnp.transpose(result, (0, 1, 3, 2))


def solution(mesh):
    placed = (
        P("row", None, None, None),
        P("row", None),
        P("row", None, None, "col"),
        P("row", None),
    )
    return jax.shard_map(
        functools.partial(body, mesh.shape["row"]),
        mesh=mesh,
        in_specs=placed,
        out_specs=P("row", None, None, "col"),
        check_vma=False,
    )
```

time: 25.8 us -> 26.1 us (1.012)
  Pallas kernels: 25 us -> 25.3 us
    pallas_call x1, Pallas kernels: 25 us -> 25.3 us  [body(): pl.pallas_call(functools.partial(kernel, row_count), out_shape=jax.ShapeD...]
where the time goes in v4:
time: 26.1 us; the launch traced here: 25.9 us
  Pallas kernels  25.3 us (97%)
  local copies, waits for them, and re-layouts  0.61 us (2%)
    pallas_call x1, Pallas kernels, body(): pl.pallas_call(functools.partial(kernel, row_count), out_shape=jax.ShapeD...  25.3 us
    unnamed x1, local copies, waits for them, and re-layouts  0.61 us

profile of v4, /device:TPU:7, one launch (start us, length us, event | category | flops | bytes accessed | tf_op | source)
XLA Modules:
  0.0 25.9 jit_solution(13762672516675304296)
XLA Ops:
  0.0 25.3 %shard_map.46 = f32[2,7,4,64]{3,2,1,0:T(4,128)S(1)} custom-call(s32[3,16]{1,0:T(4,128)} %bitcast.5, s32[16,15]{1,0:T(8,128)} %k_cols_hbm.1, f32[16,3,4,64]{3,2,1,0:T(4,128)} %bitcast.4, f32[16,15,64,64]{3,2,1,0:T(8,128)} %k_hbm.1), custom_call_target="tpu_custom_call" | custom-call | tf_op jit(solution)/shard_map/pallas_call | solution.py:473
  25.3 0.6 %copy.6 = f32[2,7,64,4]{2,3,1,0:T(4,128)} copy(f32[2,7,64,4]{2,3,1,0:T(4,128)S(1)} %bitcast.3) | data formatting | bytes 28672

commit v5 on v4

--- a/solution.py
+++ b/solution.py
@@ -229,8 +229,9 @@
                 pairs.append(jnp.concatenate([k_buf[i, s], second], axis=1))
             both = jnp.concatenate(pairs, axis=1)
             high = both.astype(BF16)
-            k_split[i, q, 0:64] = high
-            k_split[i, q, 64:128] = (both - high.astype(F32)).astype(BF16)
+            lanes = slice(256 * q, 256 * q + 256)
+            k_split[i, 0:64, lanes] = high
+            k_split[i, 64:128, lanes] = (both - high.astype(F32)).astype(BF16)
         return carry
 
     def split_part(part):
@@ -238,23 +239,27 @@
         lax.fori_loop(4 * part, 4 * part + 4, split_k, 0)
 
     def place_group(side):
-        empty = jnp.zeros((8, 128), F32)
-
         def place(m, carry):
             tiles = [[near[side, n, m * 3 + u] for u in range(3)] for n in range(4)]
             turned = [[swap_rows(tile) for tile in each] for each in tiles]
+
+            def piece(index, x, under):
+                n, u = index // 5, index % 5 - side
+                if u < 0 or u > 2:
+                    return None
+                return (tiles if x == under else turned)[n][u]
+
             for x in range(2):
                 wholes = [[], []]
-                for n in range(4):
-                    upper = turned[n] if x else tiles[n]
-                    under = tiles[n] if x else turned[n]
-                    if side == 1:
-                        found = [jnp.where(top, 0.0, under[0]), jnp.where(top, upper[1], under[2])]
+                for at in range(10):
+                    upper, under = piece(2 * at, x, 0), piece(2 * at + 1, x, 1)
+                    if upper is None and under is None:
+                        wholes[0].append(jnp.zeros((8, 128), F32))
+                        wholes[1].append(jnp.zeros((8, 128), F32))
                     else:
-                        found = [jnp.where(top, upper[0], under[1]), jnp.where(top, upper[2], 0.0)]
-                    ahead, behind = [empty] * (side // 2), [empty] * (2 - side // 2)
-                    wholes[0] += ahead + found + behind
-                    wholes[1] += ahead + [swap_lanes(tile) for tile in found] + behind
+                        tile = jnp.where(top, 0.0 if upper is None else upper, 0.0 if under is None else under)
+                        wholes[0].append(tile)
+                        wholes[1].append(swap_lanes(tile))
                 for flipped in range(2):
                     whole = jnp.concatenate(wholes[flipped], axis=0)
                     high = whole.astype(BF16)
@@ -263,23 +268,37 @@
                     table[entry_at, 1] = (whole - high.astype(F32)).astype(BF16)
             return carry
 
-        lax.fori_loop(0, 2, place, 0)
+        lax.fori_loop(0, 2, place, 0, unroll=True)
 
     split_part(0)
     split_part(1)
-    table[24:26] = jnp.zeros((2, 2, 128, 128), BF16)
+    table[24:26] = jnp.zeros((2, 2, 80, 128), BF16)
     pair_copy(0, odd * 2 + 1 - core, core, pair_peers[0]).wait_recv()
     for n in range(2):
         pair_copy(0, (1 - odd) * 2 + n, core, pair_peers[0]).wait_recv()
     place_group(1)
 
+    @pl.when(lower)
+    def _():
+        place_group(2)
+
+    @pl.when(jnp.logical_not(lower))
+    def _():
+        place_group(0)
+
     @pl.when(has_side)
     def _():
         for number in range(4):
             halo_take(number)
 
-    place_group(0)
-    place_group(2)
+    @pl.when(lower)
+    def _():
+        place_group(0)
+
+    @pl.when(jnp.logical_not(lower))
+    def _():
+        place_group(2)
+
     copies[2].wait()
 
     def entry(i, s):
@@ -290,24 +309,22 @@
         inside = (block >= 0) & (block < total_rows) & (place_of >= 0) & (place_of < 24)
         return jnp.where(inside, place_of, 24)
 
-    low_16 = lax.broadcasted_iota(jnp.int32, (128, 128), 1) < 64
+    low_16 = lax.broadcasted_iota(jnp.int32, (80, 128), 1) < 64
+    blank = jnp.zeros((48, 128), BF16)
 
     def multiply_row(i):
-        total = None
-        for q in range(4):
-            sides = []
-            for s in (4 * q, 4 * q + 2):
-                even = entry(i, s)
-                other = lax.bitwise_xor(entry(i, s + 1), 1)
-                parts = [jnp.where(low_16, table[even, part], table[other, part]) for part in range(2)]
-                sides.append(jnp.concatenate(parts, axis=0))
-            term = lax.dot_general(
-                k_split[i, q],
-                jnp.concatenate(sides, axis=1),
-                (((1,), (1,)), ((), ())),
-                preferred_element_type=F32,
-            )
-            total = term if total is None else total + term
+        sides = []
+        for s in range(0, 16, 2):
+            even = entry(i, s)
+            other = lax.bitwise_xor(entry(i, s + 1), 1)
+            parts = [jnp.where(low_16, table[even, part], table[other, part]) for part in range(2)]
+            sides.append(jnp.concatenate([parts[0], blank, parts[1], blank], axis=0))
+        total = lax.dot_general(
+            k_split[i],
+            jnp.concatenate(sides, axis=1),
+            (((1,), (1,)), ((), ())),
+            preferred_element_type=F32,
+        )
         return total[0:64, 0:128] + total[0:64, 128:256] + total[64:128, 0:128]
 
     def multiply(n, carry):
@@ -320,7 +337,7 @@
             weights[rows, 256 + 128 * x : 384 + 128 * x] = (value - high.astype(F32)).astype(BF16)
         return carry
 
-    lax.fori_loop(0, 4, multiply, 0)
+    lax.fori_loop(0, 4, multiply, 0, unroll=True)
 
     def prepare(place_at, slot):
         for part in range(2):
@@ -334,6 +351,17 @@
             rest = whole - whole.astype(BF16).astype(F32)
             rows = pl.ds(96 * place_at + 48 * part, 48)
             left_side[rows] = jnp.concatenate([whole, rest], axis=0).astype(BF16)
+
+    lane = lax.broadcasted_iota(jnp.int32, (8, 128), 1)
+    lane_group = lane // 32
+
+    def spread(value, u):
+        start = 8 - 4 * u
+        moved = [pltpu.roll(value, start + 12 * n, 1) if start + 12 * n else value for n in range(4)]
+        first = jnp.where(lane_group == 0, moved[0], moved[1])
+        second = jnp.where(lane_group == 2, moved[2], moved[3])
+        within = lane % 32 - start
+        return jnp.where((within >= 0) & (within < 20), jnp.where(lane < 64, first, second), 0.0)
 
     def products(first, slots):
         count = len(slots)
@@ -353,7 +381,7 @@
                     folded.append(jnp.where(top, value[:, 0:128], value[:, 128:256]))
                 value = jnp.where(top, folded[0], folded[1])
                 value = value + swap_rows(jnp.where(top, folded[1], folded[0]))
-                terms[u, slot] = value if u == 2 else pltpu.roll(value, 8 - 4 * u, 1)
+                terms[u, slot] = spread(value, u)
 
     early, late = (0, 1), (2, 3)
     for part in range(2):
@@ -366,8 +394,6 @@
             take(slot, part)
         prepare(2 + n, slot)
     products(2, late)
-
-    lane_group = lax.broadcasted_iota(jnp.int32, (8, 128), 1) // 32
 
     def rotate(value, groups):
         return value if groups % 4 == 0 else pltpu.roll(value, 32 * (groups % 4), 1)
@@ -480,10 +506,10 @@
             pltpu.SMEM((own, 15), jnp.int32),
             pltpu.VMEM((own, 3, 4, 64), F32),
             pltpu.VMEM((AGG, 15, 64, 64), F32),
-            pltpu.VMEM((AGG, 4, 128, 256), BF16),
+            pltpu.VMEM((AGG, 128, 1024), BF16),
             pltpu.VMEM((3, 4, 6, 8, 128), F32),
             pltpu.VMEM((3, 2, 6, 8, 128), F32),
-            pltpu.VMEM((26, 2, 128, 128), BF16),
+            pltpu.VMEM((26, 2, 80, 128), BF16),
             pltpu.VMEM((256, 512), BF16),
             pltpu.VMEM((384, 256), BF16),
             pltpu.VMEM((3, 4, 8, 128), F32),

time: 26.1 us -> 25.1 us (0.962)
  Pallas kernels: 25.3 us -> 24.4 us
    pallas_call x1, Pallas kernels: 25.3 us -> 24.4 us  [body(): pl.pallas_call(functools.partial(kernel, row_count), out_shape=jax.ShapeD...]
where the time goes in v5:
time: 25.1 us; the launch traced here: 25 us
  Pallas kernels  24.4 us (97%)
  local copies, waits for them, and re-layouts  0.61 us (2%)
    pallas_call x1, Pallas kernels, body(): pl.pallas_call(functools.partial(kernel, row_count), out_shape=jax.ShapeD...  24.4 us
    unnamed x1, local copies, waits for them, and re-layouts  0.61 us

profile of v5, /device:TPU:7, one launch (start us, length us, event | category | flops | bytes accessed | tf_op | source)
XLA Modules:
  0.0 25.0 jit_solution(17398714043213061490)
XLA Ops:
  0.0 24.4 %shard_map.46 = f32[2,7,4,64]{3,2,1,0:T(4,128)S(1)} custom-call(s32[3,16]{1,0:T(4,128)} %bitcast.5, s32[16,15]{1,0:T(8,128)} %k_cols_hbm.1, f32[16,3,4,64]{3,2,1,0:T(4,128)} %bitcast.4, f32[16,15,64,64]{3,2,1,0:T(8,128)} %k_hbm.1), custom_call_target="tpu_custom_call" | custom-call | tf_op jit(solution)/shard_map/pallas_call | solution.py:499
  24.4 0.6 %copy.6 = f32[2,7,64,4]{2,3,1,0:T(4,128)} copy(f32[2,7,64,4]{2,3,1,0:T(4,128)S(1)} %bitcast.3) | data formatting | bytes 28672

commit v6 on v5

--- a/solution.py
+++ b/solution.py
@@ -31,7 +31,6 @@
     ring,
     table,
     weights,
-    left_side,
     terms,
     packed,
     pair_in,
@@ -339,7 +338,8 @@
 
     lax.fori_loop(0, 4, multiply, 0, unroll=True)
 
-    def prepare(place_at, slot):
+    def prepare(slot):
+        parts = []
         for part in range(2):
 
             def tile(m, u):
@@ -348,9 +348,8 @@
             whole = jnp.concatenate(
                 [jnp.concatenate([tile(m, u) for m in range(2)], axis=1) for u in range(3)], axis=0
             )
-            rest = whole - whole.astype(BF16).astype(F32)
-            rows = pl.ds(96 * place_at + 48 * part, 48)
-            left_side[rows] = jnp.concatenate([whole, rest], axis=0).astype(BF16)
+            parts += [whole, whole - whole.astype(BF16).astype(F32)]
+        return jnp.concatenate(parts, axis=0).astype(BF16)
 
     lane = lax.broadcasted_iota(jnp.int32, (8, 128), 1)
     lane_group = lane // 32
@@ -363,10 +362,9 @@
         within = lane % 32 - start
         return jnp.where((within >= 0) & (within < 20), jnp.where(lane < 64, first, second), 0.0)
 
-    def products(first, slots):
-        count = len(slots)
+    def products(slots, factors):
         result = lax.dot_general(
-            left_side[pl.ds(96 * first, 96 * count)],
+            jnp.concatenate(factors, axis=0),
             weights[...],
             (((1,), (0,)), ((), ())),
             preferred_element_type=F32,
@@ -383,28 +381,27 @@
                 value = value + swap_rows(jnp.where(top, folded[1], folded[0]))
                 terms[u, slot] = spread(value, u)
 
-    early, late = (0, 1), (2, 3)
-    for part in range(2):
-        take(1, part)
-    for n, slot in enumerate(early):
-        prepare(n, slot)
-    products(0, early)
-    for n, slot in enumerate(late):
+    factors = []
+    for slot in range(4):
         for part in range(2):
-            take(slot, part)
-        prepare(2 + n, slot)
-    products(2, late)
+            if slot > 0:
+                take(slot, part)
+        factors.append(prepare(slot))
+    products((0, 1, 2, 3), factors)
 
     def rotate(value, groups):
         return value if groups % 4 == 0 else pltpu.roll(value, 32 * (groups % 4), 1)
 
-    for u in (0, 2, 1):
+    def pack(u):
         parts = [terms[u, slot] for slot in range(4)]
         for number in range(4):
             moved = [rotate(parts[slot], slot - number) for slot in range(4)]
             left_half = jnp.where(lane_group == 0, moved[0], moved[1])
             right_half = jnp.where(lane_group == 2, moved[2], moved[3])
             packed[number, u] = jnp.where(low, left_half, right_half)
+
+    pack(0)
+    pack(2)
 
     def side_copy(number):
         return pltpu.make_async_remote_copy(
@@ -430,6 +427,8 @@
     def _():
         for number in range(4):
             side_copy(number).start()
+
+    pack(1)
 
     def last_copy(n, number, chip, which, peer):
         return pltpu.make_async_remote_copy(
@@ -511,7 +510,6 @@
             pltpu.VMEM((3, 2, 6, 8, 128), F32),
             pltpu.VMEM((26, 2, 80, 128), BF16),
             pltpu.VMEM((256, 512), BF16),
-            pltpu.VMEM((384, 256), BF16),
             pltpu.VMEM((3, 4, 8, 128), F32),
             pltpu.VMEM((4, 3, 8, 128), F32),
             pltpu.VMEM((2, 2, 2, 8, 128), F32),

time: 25.1 us -> 24.8 us (0.988)
  Pallas kernels: 24.4 us -> 24.1 us
    pallas_call x1, Pallas kernels: 24.4 us -> 24.1 us  [body(): pl.pallas_call(functools.partial(kernel, row_count), out_shape=jax.ShapeD...]
where the time goes in v6:
time: 24.8 us; the launch traced here: 24.7 us
  Pallas kernels  24.1 us (97%)
  local copies, waits for them, and re-layouts  0.61 us (2%)
    pallas_call x1, Pallas kernels, body(): pl.pallas_call(functools.partial(kernel, row_count), out_shape=jax.ShapeD...  24.1 us
    unnamed x1, local copies, waits for them, and re-layouts  0.61 us

profile of v6, /device:TPU:7, one launch (start us, length us, event | category | flops | bytes accessed | tf_op | source)
XLA Modules:
  0.0 24.7 jit_solution(17786706437949659078)
XLA Ops:
  0.0 24.1 %shard_map.46 = f32[2,7,4,64]{3,2,1,0:T(4,128)S(1)} custom-call(s32[3,16]{1,0:T(4,128)} %bitcast.5, s32[16,15]{1,0:T(8,128)} %k_cols_hbm.1, f32[16,3,4,64]{3,2,1,0:T(4,128)} %bitcast.4, f32[16,15,64,64]{3,2,1,0:T(8,128)} %k_hbm.1), custom_call_target="tpu_custom_call" | custom-call | tf_op jit(solution)/shard_map/pallas_call | solution.py:498
  24.1 0.6 %copy.6 = f32[2,7,64,4]{2,3,1,0:T(4,128)} copy(f32[2,7,64,4]{2,3,1,0:T(4,128)S(1)} %bitcast.3) | data formatting | bytes 28672

commit v7 on v6

--- a/solution.py
+++ b/solution.py
@@ -326,30 +326,30 @@
         )
         return total[0:64, 0:128] + total[0:64, 128:256] + total[64:128, 0:128]
 
-    def multiply(n, carry):
-        i = n + 2 * (n // 2)
-        rows = pl.ds(pl.multiple_of(64 * n, 64), 64)
-        for x in range(2):
-            value = multiply_row(i + 2 * x)
-            high = value.astype(BF16)
-            weights[rows, 128 * x : 128 * x + 128] = high
-            weights[rows, 256 + 128 * x : 384 + 128 * x] = (value - high.astype(F32)).astype(BF16)
+    def multiply(i, carry):
+        rows = pl.ds(pl.multiple_of(64 * i, 64), 64)
+        value = multiply_row(i)
+        high = value.astype(BF16)
+        weights[rows, 0:128] = high
+        weights[rows, 128:256] = (value - high.astype(F32)).astype(BF16)
         return carry
 
-    lax.fori_loop(0, 4, multiply, 0, unroll=True)
+    lax.fori_loop(0, AGG, multiply, 0, unroll=True)
+
+    def merge(zero, one):
+        mixed = swap_rows(jnp.where(top, one, zero))
+        return [jnp.where(top, zero, mixed), jnp.where(top, mixed, one)]
 
     def prepare(slot):
-        parts = []
-        for part in range(2):
-
-            def tile(m, u):
-                return near[1, odd * 2 + part, m * 3 + u] if slot == 0 else ring[slot - 1, part, m * 3 + u]
-
-            whole = jnp.concatenate(
-                [jnp.concatenate([tile(m, u) for m in range(2)], axis=1) for u in range(3)], axis=0
-            )
-            parts += [whole, whole - whole.astype(BF16).astype(F32)]
-        return jnp.concatenate(parts, axis=0).astype(BF16)
+        def tile(part, at):
+            return near[1, odd * 2 + part, at] if slot == 0 else ring[slot - 1, part, at]
+
+        rows = []
+        for u in range(3):
+            pieces = merge(tile(0, u), tile(1, u)) + merge(tile(0, 3 + u), tile(1, 3 + u))
+            rows.append(jnp.concatenate(pieces, axis=1))
+        whole = jnp.concatenate(rows, axis=0)
+        return jnp.concatenate([whole, whole - whole.astype(BF16).astype(F32)], axis=0).astype(BF16)
 
     lane = lax.broadcasted_iota(jnp.int32, (8, 128), 1)
     lane_group = lane // 32
@@ -371,14 +371,8 @@
         )
         for n, slot in enumerate(slots):
             for u in range(3):
-                folded = []
-                for part in range(2):
-                    a = 96 * n + 48 * part + 8 * u
-                    value = result[a : a + 8, 0:256] + result[a : a + 8, 256:512]
-                    value = value + result[a + 24 : a + 32, 0:256]
-                    folded.append(jnp.where(top, value[:, 0:128], value[:, 128:256]))
-                value = jnp.where(top, folded[0], folded[1])
-                value = value + swap_rows(jnp.where(top, folded[1], folded[0]))
+                a = 48 * n + 8 * u
+                value = result[a : a + 8, 0:128] + result[a : a + 8, 128:256] + result[a + 24 : a + 32, 0:128]
                 terms[u, slot] = spread(value, u)
 
     factors = []
@@ -509,7 +503,7 @@
             pltpu.VMEM((3, 4, 6, 8, 128), F32),
             pltpu.VMEM((3, 2, 6, 8, 128), F32),
             pltpu.VMEM((26, 2, 80, 128), BF16),
-            pltpu.VMEM((256, 512), BF16),
+            pltpu.VMEM((512, 256), BF16),
             pltpu.VMEM((3, 4, 8, 128), F32),
             pltpu.VMEM((4, 3, 8, 128), F32),
             pltpu.VMEM((2, 2, 2, 8, 128), F32),

time: 24.8 us -> 24.8 us (level)
  no operation moved by 1% of the time
where the time goes in v7:
time: 24.8 us; the launch traced here: 24.7 us
  Pallas kernels  24 us (97%)
  local copies, waits for them, and re-layouts  0.61 us (2%)
    pallas_call x1, Pallas kernels, body(): pl.pallas_call(functools.partial(kernel, row_count), out_shape=jax.ShapeD...  24 us
    unnamed x1, local copies, waits for them, and re-layouts  0.61 us

profile of v7, /device:TPU:7, one launch (start us, length us, event | category | flops | bytes accessed | tf_op | source)
XLA Modules:
  0.0 24.7 jit_solution(6475380494956504397)
XLA Ops:
  0.0 24.0 %shard_map.46 = f32[2,7,4,64]{3,2,1,0:T(4,128)S(1)} custom-call(s32[3,16]{1,0:T(4,128)} %bitcast.5, s32[16,15]{1,0:T(8,128)} %k_cols_hbm.1, f32[16,3,4,64]{3,2,1,0:T(4,128)} %bitcast.4, f32[16,15,64,64]{3,2,1,0:T(8,128)} %k_hbm.1), custom_call_target="tpu_custom_call" | custom-call | tf_op jit(solution)/shard_map/pallas_call | solution.py:492
  24.0 0.6 %copy.6 = f32[2,7,64,4]{2,3,1,0:T(4,128)} copy(f32[2,7,64,4]{2,3,1,0:T(4,128)S(1)} %bitcast.3) | data formatting | bytes 28672

commit v8 on v7

--- a/solution.py
+++ b/solution.py
@@ -235,7 +235,7 @@
 
     def split_part(part):
         k_copies[part].wait()
-        lax.fori_loop(4 * part, 4 * part + 4, split_k, 0)
+        lax.fori_loop(4 * part, 4 * part + 4, split_k, 0, unroll=True)
 
     def place_group(side):
         def place(m, carry):
@@ -285,6 +285,23 @@
     def _():
         place_group(0)
 
+    def merge(zero, one):
+        mixed = swap_rows(jnp.where(top, one, zero))
+        return [jnp.where(top, zero, mixed), jnp.where(top, mixed, one)]
+
+    def prepare(slot):
+        def tile(part, at):
+            return near[1, odd * 2 + part, at] if slot == 0 else ring[slot - 1, part, at]
+
+        rows = []
+        for u in range(3):
+            pieces = merge(tile(0, u), tile(1, u)) + merge(tile(0, 3 + u), tile(1, 3 + u))
+            rows.append(jnp.concatenate(pieces, axis=1))
+        whole = jnp.concatenate(rows, axis=0)
+        return jnp.concatenate([whole, whole - whole.astype(BF16).astype(F32)], axis=0).astype(BF16)
+
+    own_factor = prepare(0)
+
     @pl.when(has_side)
     def _():
         for number in range(4):
@@ -336,21 +353,6 @@
 
     lax.fori_loop(0, AGG, multiply, 0, unroll=True)
 
-    def merge(zero, one):
-        mixed = swap_rows(jnp.where(top, one, zero))
-        return [jnp.where(top, zero, mixed), jnp.where(top, mixed, one)]
-
-    def prepare(slot):
-        def tile(part, at):
-            return near[1, odd * 2 + part, at] if slot == 0 else ring[slot - 1, part, at]
-
-        rows = []
-        for u in range(3):
-            pieces = merge(tile(0, u), tile(1, u)) + merge(tile(0, 3 + u), tile(1, 3 + u))
-            rows.append(jnp.concatenate(pieces, axis=1))
-        whole = jnp.concatenate(rows, axis=0)
-        return jnp.concatenate([whole, whole - whole.astype(BF16).astype(F32)], axis=0).astype(BF16)
-
     lane = lax.broadcasted_iota(jnp.int32, (8, 128), 1)
     lane_group = lane // 32
 
@@ -375,11 +377,10 @@
                 value = result[a : a + 8, 0:128] + result[a : a + 8, 128:256] + result[a + 24 : a + 32, 0:128]
                 terms[u, slot] = spread(value, u)
 
-    factors = []
-    for slot in range(4):
+    factors = [own_factor]
+    for slot in range(1, 4):
         for part in range(2):
-            if slot > 0:
-                take(slot, part)
+            take(slot, part)
         factors.append(prepare(slot))
     products((0, 1, 2, 3), factors)
 

time: 24.8 us -> 24.8 us (level)
  no operation moved by 1% of the time
where the time goes in v8:
time: 24.8 us; the launch traced here: 24.7 us
  Pallas kernels  24 us (97%)
  local copies, waits for them, and re-layouts  0.61 us (2%)
    pallas_call x1, Pallas kernels, body(): pl.pallas_call(functools.partial(kernel, row_count), out_shape=jax.ShapeD...  24 us
    unnamed x1, local copies, waits for them, and re-layouts  0.61 us

profile of v8, /device:TPU:7, one launch (start us, length us, event | category | flops | bytes accessed | tf_op | source)
XLA Modules:
  0.0 24.7 jit_solution(17761620588449104829)
XLA Ops:
  0.0 24.0 %shard_map.46 = f32[2,7,4,64]{3,2,1,0:T(4,128)S(1)} custom-call(s32[3,16]{1,0:T(4,128)} %bitcast.5, s32[16,15]{1,0:T(8,128)} %k_cols_hbm.1, f32[16,3,4,64]{3,2,1,0:T(4,128)} %bitcast.4, f32[16,15,64,64]{3,2,1,0:T(8,128)} %k_hbm.1), custom_call_target="tpu_custom_call" | custom-call | tf_op jit(solution)/shard_map/pallas_call | solution.py:493
  24.1 0.6 %copy.6 = f32[2,7,64,4]{2,3,1,0:T(4,128)} copy(f32[2,7,64,4]{2,3,1,0:T(4,128)S(1)} %bitcast.3) | data formatting | bytes 28672

commit v9 on v8

--- a/solution.py
+++ b/solution.py
@@ -435,7 +435,7 @@
             device_id_type=MESH,
         )
 
-    for n, peer in enumerate(pair_peers):
+    for n, peer in ((1, pair_peers[1]), (2, pair_peers[2]), (0, pair_peers[0])):
         number = odd * 2 + 1 - core if n == 0 else (1 - odd) * 2 + n - 1
         started.append(last_copy(n, number, odd, core, peer))
         started[-1].start()

time: 24.8 us -> 24.8 us (level)
  no operation moved by 1% of the time
where the time goes in v9:
time: 24.8 us; the launch traced here: 24.7 us
  Pallas kernels  24 us (97%)
  local copies, waits for them, and re-layouts  0.61 us (2%)
    pallas_call x1, Pallas kernels, body(): pl.pallas_call(functools.partial(kernel, row_count), out_shape=jax.ShapeD...  24 us
    unnamed x1, local copies, waits for them, and re-layouts  0.61 us

profile of v9, /device:TPU:7, one launch (start us, length us, event | category | flops | bytes accessed | tf_op | source)
XLA Modules:
  0.0 24.7 jit_solution(10124262954218624038)
XLA Ops:
  0.0 24.0 %shard_map.46 = f32[2,7,4,64]{3,2,1,0:T(4,128)S(1)} custom-call(s32[3,16]{1,0:T(4,128)} %bitcast.5, s32[16,15]{1,0:T(8,128)} %k_cols_hbm.1, f32[16,3,4,64]{3,2,1,0:T(4,128)} %bitcast.4, f32[16,15,64,64]{3,2,1,0:T(8,128)} %k_hbm.1), custom_call_target="tpu_custom_call" | custom-call | tf_op jit(solution)/shard_map/pallas_call | solution.py:493
  24.1 0.6 %copy.6 = f32[2,7,64,4]{2,3,1,0:T(4,128)} copy(f32[2,7,64,4]{2,3,1,0:T(4,128)S(1)} %bitcast.3) | data formatting | bytes 28672
